TPU v7x, 256 devices: a whole 4x4x8 slice. The times are simulated.
256 devices in a mesh: pitch: 16 (over z, core), span: 16 (over y, x).
Axes of the slice: x: 4, y: 4, z: 8, core: 2. Of those that a mesh axis runs over, the one named last changes fastest.
Arguments:
- blocks: bfloat16 [16384, 80, 880], P(('pitch', 'span'))
- columns: int32 [16384, 11], P(('pitch', 'span')), may hold values from 0 to 95, as said below
- margin_columns: int32 [8192, 4], P(('pitch', 'span')), may hold values from 0 to 96, as said below
- send_lists: int32 [1024, 8], P(('pitch', 'span')), may hold values from 0 to 63, as said below
- basis: bfloat16 [8, 16384, 80], P(None, ('pitch', 'span')), as said below
Outputs:
- new_vector: bfloat16 [16384, 80], P(('pitch', 'span'))
- projections: float32 [9], replicated
Inputs may be any that keep to these rules, and one draw needn't show every extreme that they name: `columns`: slot 0 of each face's row is the face's own index among its subdomain's 64 faces; the other slots hold distinct indices into the intersected subdomain, all different from the face's own index. `margin_columns`: slot 0 of margin face g's row is its own position 64 + g; the other slots hold distinct positions in the intersected subdomain other than its own, or 96 for a dropped coupling. `send_lists`: each row holds 8 distinct faces of its subdomain. `basis`: the vectors are orthonormal under <a, b> up to bfloat16 rounding.
All inputs are finite; a program needn't handle non-finite values.
Results may differ from a plain program's by a relative error of at most 0.03.
The roundings to bfloat16 on the way count: a program that leaves them out, or rounds other values in their place, can miss the bound.
Values may be sent and summed in bfloat16 or wider, within the bound.
No kernel may reach another device: no remote copies, remote signals or barrier semaphores. Data moves between devices by JAX's collectives and lax.ppermute only.
A program may use at most 128 MiB of HBM per device.

v0:
```python
import jax
import jax.numpy as jnp
from jax import lax
from jax.sharding import PartitionSpec as P

BLOCK = 80
SLOTS = 11
GSLOTS = 4
F_DEV = 64
KRYLOV = 8
SWEEPS = 4
LIST = 8


center_value = 1.0
half_width = 0.5
epsilon = 1e-06


def shifted(value, axis, by):
    devices = lax.axis_size(axis)
    return lax.ppermute(value, axis, [(i, (i + by) % devices) for i in range(devices)])


def shifted_2(value, axis, by):
    devices = lax.axis_size(axis)
    pairs = [(i, i + by) for i in range(devices) if 0 <= i + by < devices]
    return lax.ppermute(value, axis, pairs)


def forward_rows(outgoing):
    received = []
    for offset, list_index in ((1, 0), (-1, 1)):
        received.append(shifted(outgoing[list_index], "pitch", offset))
    for offset, list_index in ((1, 2), (-1, 3)):
        received.append(shifted_2(outgoing[list_index], "span", offset))
    return jnp.concatenate(received, axis=0)


def forward_values(outgoing):
    received = []
    for offset, list_index in ((1, 0), (-1, 1)):
        received.append(shifted(outgoing[list_index], "pitch", offset))
    for offset, list_index in ((1, 2), (-1, 3)):
        received.append(shifted_2(outgoing[list_index], "span", offset))
    return jnp.concatenate(received, axis=0)


def own_rows(block_rows, column_ids, extended):
    gathered = extended[column_ids].reshape(column_ids.shape[0], SLOTS * BLOCK)
    return jnp.einsum("fij,fj->fi", block_rows, gathered, preferred_element_type=jnp.float32)


def margin_rows(row_blocks, margin_ids, padded):
    gathered = padded[margin_ids].reshape(margin_ids.shape[0], GSLOTS * BLOCK)
    return jnp.einsum("gij,gj->gi", row_blocks, gathered, preferred_element_type=jnp.float32)


def sweep_constants():
    stretch = center_value / half_width
    ratio_now = 1.0 / stretch
    factors = []
    for sweep_index in range(SWEEPS - 1):
        ratio_next = 1.0 / (2.0 * stretch - ratio_now)
        factors.append((ratio_next * ratio_now, 2.0 * ratio_next / half_width))
        ratio_now = ratio_next
    return factors


def per_device(blocks, columns, margin_columns, send_lists, basis):
    latest = basis[KRYLOV - 1]
    factors = sweep_constants()
    flat_rows = send_lists.reshape(4 * LIST)
    leading = blocks[flat_rows, :, : GSLOTS * BLOCK]
    padded_values = jnp.pad(latest[flat_rows], ((0, 0), (0, GSLOTS * BLOCK - BLOCK)))
    packed = jnp.concatenate([leading, padded_values[:, None, :]], axis=1)
    arrived = forward_rows(packed.reshape(4, LIST, BLOCK + 1, GSLOTS * BLOCK))
    arrived_blocks = arrived[:, :BLOCK]
    ghost_values = arrived[:, BLOCK, :BLOCK]
    residual = jnp.concatenate([latest, ghost_values], axis=0).astype(jnp.float32)
    direction = residual / center_value
    solution = jnp.zeros_like(residual)
    zero_row = jnp.zeros((1, BLOCK), jnp.bfloat16)
    for sweep_index in range(SWEEPS):
        solution = solution + direction
        if sweep_index < SWEEPS - 1:
            rounded = direction.astype(jnp.bfloat16)
            padded = jnp.concatenate([rounded, zero_row], axis=0)
            applied = jnp.concatenate(
                [
                    own_rows(blocks, columns, rounded),
                    margin_rows(arrived_blocks, margin_columns, padded),
                ],
                axis=0,
            )
            residual = residual - applied
            keep_factor, push_factor = factors[sweep_index]
            direction = keep_factor * direction + push_factor * residual
    precond = solution[:F_DEV].astype(jnp.bfloat16)
    extended = jnp.concatenate([precond, forward_values(precond[send_lists])], axis=0)
    image = own_rows(blocks, columns, extended)
    inverse_count = 1.0 / (lax.axis_size("pitch") * lax.axis_size("span") * F_DEV * BLOCK)
    basis_wide = basis.astype(jnp.float32)
    local_heights = jnp.sum(basis_wide * image[None], axis=(1, 2))
    heights = lax.psum(local_heights, ("pitch", "span")) * inverse_count
    remainder = image - jnp.tensordot(heights, basis_wide, axes=1, precision=lax.Precision.HIGHEST)
    squares = lax.psum(jnp.sum(remainder * remainder), ("pitch", "span")) * inverse_count
    length_value = jnp.sqrt(squares + epsilon)
    new_vector = (remainder / length_value).astype(jnp.bfloat16)
    return (new_vector, jnp.concatenate([heights, length_value[None]]))


def solution(mesh):
    return jax.shard_map(
        per_device,
        mesh=mesh,
        in_specs=(
            P(("pitch", "span"), None, None),
            P(("pitch", "span"), None),
            P(("pitch", "span"), None),
            P(("pitch", "span"), None),
            P(None, ("pitch", "span"), None),
        ),
        out_specs=(P(("pitch", "span"), None), P()),
        check_vma=False,
    )
```

profile of v0, /device:TPU:1, one launch (start us, length us, event | category | flops | bytes accessed | tf_op | source)
XLA Modules:
  0.0 277.1 jit_solution(938073077386945855)
XLA Ops:
  0.6 0.7 slice_bitcast_fusion
  1.4 0.8 reshape.66
  2.1 0.7 compare_select_fusion
  3.1 0.6 gather_fusion.1
  3.7 2.7 copy.17
  6.4 18.9 %copy.16 = bf16[64,80,880]{1,0,2:T(8,128)(2,1)} copy(bf16[64,80,880]{2,1,0:T(8,128)(2,1)} %param.5) | data formatting | bytes 18022400 | tf_op args[0]
  25.3 11.4 %gather_fusion = bf16[32,80,320]{1,0,2:T(8,128)(2,1)} fusion(bf16[64,80,880]{1,0,2:T(8,128)(2,1)} %copy.16, s32[32]{0:T(128)S(1)} %get-tuple-element.22), kind=kCustom, calls=%fused_computation | custom fusion | bytes 3277056 | tf_op jit(solution)/shard_map/gather | solution.py:74
  36.7 4.4 %pad_maximum_fusion = (bf16[8,81,320]{1,0,2:T(8,128)(2,1)S(1)}, bf16[8,81,320]{1,0,2:T(8,128)(2,1)}, bf16[8,81,320]{1,0,2:T(8,128)(2,1)}, bf16[8,81,320]{1,0,2:T(8,128)(2,1)}) fusion(bf16[32,1,320]{1,0,2:T(8,128)(2,1)S(1)} %copy.17, bf16[32,80,320]{1,0,2:T(8,128)(2,1)} %gather_fusion), kind=kLoop, calls=%fused_computation.25 | loop fusion | flops 3317760 | bytes 3317760 | tf_op jit(solution)/shard_map/concatenate | solution.py:76
  41.1 2.6 copy.18
  43.7 3.0 %collective-permute-start = (bf16[8,81,320]{2,0,1:T(8,128)(2,1)}, bf16[8,81,320]{2,0,1:T(8,128)(2,1)}, u32[]{:S(2)}, u32[]{:S(2)}) collective-permute-start(bf16[8,81,320]{2,0,1:T(8,128)(2,1)} %copy.18), channel_id=1, source_target_pairs={{0,16},{16,32},{32,48},{48,64},{64,80},{80,96},{96,112},{112,128},... | collective-permute-start | bytes 1244168 | tf_op jit(solution)/shard_map/ppermute | solution.py:22
  46.7 2.5 copy.19
  49.5 0.6 copy.20
  50.1 2.9 %collective-permute-start.2 = (bf16[8,81,320]{2,0,1:T(8,128)(2,1)S(1)}, bf16[8,81,320]{2,0,1:T(8,128)(2,1)S(1)}, u32[]{:S(2)}, u32[]{:S(2)}) collective-permute-start(bf16[8,81,320]{2,0,1:T(8,128)(2,1)S(1)} %copy.20), channel_id=1, source_target_pairs={{0,1},{1,2},{2,3},{3,4},{4,5},{5,6},{6,7},{7,8},{8,9},{9,10},{10,1... | collective-permute-start | bytes 1244168 | tf_op jit(solution)/shard_map/ppermute | solution.py:28
  53.0 0.6 copy.21
  53.6 1.5 collective-permute-start.3
  55.5 1.1 constant_dynamic-update-slice_fusion.3
  56.5 1.3 collective-permute-done.1
  57.9 1.1 constant_dynamic-update-slice_fusion.2
  59.0 0.8 collective-permute-done.2
  59.9 4.4 %collective-permute-done.3 = bf16[8,81,320]{2,0,1:T(8,128)(2,1)S(1)} collective-permute-done((bf16[8,81,320]{2,0,1:T(8,128)(2,1)S(1)}, bf16[8,81,320]{2,0,1:T(8,128)(2,1)S(1)}, u32[]{:S(2)}, u32[]{:S(2)}) %collective-permute-start.3) | collective-permute-done | bytes 414752 | tf_op jit(solution)/shard_map/ppermute | solution.py:28
  64.6 0.7 gather_fusion.3
  65.5 2.0 gather_fusion.2
  67.5 0.3 reshape.200
  67.8 6.4 %fusion.23 = f32[64,1,80]{2,1,0:T(1,128)S(1)} fusion(bf16[64,880,1]{1,2,0:T(2,128)(2,1)S(1)} %reshape.200, bf16[64,80,880]{2,1,0:T(8,128)(2,1)} %param.5), kind=kOutput, calls=%fused_computation.73 | convolution fusion | flops 9011200 | bytes 9144320 | tf_op jit(solution)/shard_map/fij,fj->fi/dot_general | solution.py:51
  74.2 0.8 fusion.4
  75.0 2.0 gather_fusion.4
  77.1 0.3 reshape.204
  77.4 6.4 %fusion.24 = f32[64,1,80]{2,1,0:T(1,128)S(1)} fusion(bf16[64,880,1]{1,2,0:T(2,128)(2,1)S(1)} %reshape.204, bf16[64,80,880]{2,1,0:T(8,128)(2,1)} %param.5), kind=kOutput, calls=%fused_computation.74 | convolution fusion | flops 9011200 | bytes 9144320 | tf_op jit(solution)/shard_map/fij,fj->fi/dot_general | solution.py:51
  83.8 0.7 gather_fusion.5
  84.7 0.8 fusion.2
  85.5 2.0 gather_fusion.6
  87.5 0.3 reshape.208
  87.9 6.4 %fusion.25 = f32[64,1,80]{2,1,0:T(1,128)S(1)} fusion(bf16[64,880,1]{1,2,0:T(2,128)(2,1)S(1)} %reshape.208, bf16[64,80,880]{2,1,0:T(8,128)(2,1)} %param.5), kind=kOutput, calls=%fused_computation.75 | convolution fusion | flops 9011200 | bytes 9144320 | tf_op jit(solution)/shard_map/fij,fj->fi/dot_general | solution.py:51
  94.2 0.7 gather_fusion.7
  95.1 0.8 fusion
  95.9 0.6 gather_fusion.8
  96.5 6.5 %collective-permute-start.4 = (bf16[8,80]{1,0:T(8,128)(2,1)S(1)}, bf16[8,80]{1,0:T(8,128)(2,1)S(1)}, u32[]{:S(2)}, u32[]{:S(2)}) collective-permute-start(bf16[8,80]{1,0:T(8,128)(2,1)S(1)} %get-tuple-element.20), channel_id=1, source_target_pairs={{0,16},{16,32},{32,48},{48,64},{64,80},{80,96},{96,112},{112,128},... | collective-permute-start | bytes 3848 | tf_op jit(solution)/shard_map/ppermute | solution.py:22
  103.1 3.1 %collective-permute-start.6 = (bf16[8,80]{1,0:T(8,128)(2,1)S(1)}, bf16[8,80]{1,0:T(8,128)(2,1)S(1)}, u32[]{:S(2)}, u32[]{:S(2)}) collective-permute-start(bf16[8,80]{1,0:T(8,128)(2,1)S(1)} %get-tuple-element.18), channel_id=1, source_target_pairs={{0,1},{1,2},{2,3},{3,4},{4,5},{5,6},{6,7},{7,8},{8,9},{9,10},{10,1... | collective-permute-start | bytes 3848 | tf_op jit(solution)/shard_map/ppermute | solution.py:28
  106.1 1.3 collective-permute-start.7
  107.5 3.0 %collective-permute-done.7 = bf16[8,80]{1,0:T(8,128)(2,1)S(1)} collective-permute-done((bf16[8,80]{1,0:T(8,128)(2,1)S(1)}, bf16[8,80]{1,0:T(8,128)(2,1)S(1)}, u32[]{:S(2)}, u32[]{:S(2)}) %collective-permute-start.7) | collective-permute-done | bytes 1312 | tf_op jit(solution)/shard_map/ppermute | solution.py:28
  110.5 2.0 gather_fusion.9
  112.5 0.3 reshape.212
  112.8 6.4 %fusion.26 = f32[64,1,80]{2,1,0:T(1,128)S(1)} fusion(bf16[64,880,1]{1,2,0:T(2,128)(2,1)S(1)} %reshape.212, bf16[64,80,880]{2,1,0:T(8,128)(2,1)} %param.5), kind=kOutput, calls=%fused_computation.76 | convolution fusion | flops 9011200 | bytes 9144320 | tf_op jit(solution)/shard_map/fij,fj->fi/dot_general | solution.py:51
  119.4 80.9 %psum.14 = f32[8]{0:T(128)S(1)} all-reduce(f32[8]{0:T(128)S(1)} %multiply_reduce_fusion), channel_id=1, replica_groups=mesh['pitch'=16,'span'=16] {'pitch','span'}, use_global_device_ids=true, to_apply=%region_1.2 | all-reduce | flops 8 | bytes 64 | tf_op jit(solution)/shard_map/psum | solution.py:105
  200.6 0.6 multiply_reduce_fusion.1
  201.2 74.0 %psum.15 = f32[]{:T(128)} all-reduce(f32[]{:T(128)} %get-tuple-element.2), channel_id=1, replica_groups=mesh['pitch'=16,'span'=16] {'pitch','span'}, use_global_device_ids=true, to_apply=%region_3.4 | all-reduce | flops 1 | bytes 8 | tf_op jit(solution)/shard_map/psum | solution.py:107
  275.9 0.6 divide_convert_fusion
  276.5 0.6 pad_maximum_fusion.3
  (47 shorter events, 2.1 us)
Async XLA Ops:
  41.1 8.4 %copy-start = (bf16[8,81,320]{1,0,2:T(8,128)(2,1)S(1)}, bf16[8,81,320]{1,0,2:T(8,128)(2,1)}, u32[]{:S(2)}) copy-start(bf16[8,81,320]{1,0,2:T(8,128)(2,1)} %get-tuple-element.14) | copy-start | bytes 1244164
  43.7 11.4 %copy-start.2 = (s32[4,8]{1,0:T(4,128)S(1)}, s32[4,8]{1,0:T(4,128)}, u32[]{:S(2)}) copy-start(s32[4,8]{1,0:T(4,128)} %param.8) | copy-start | bytes 388
  43.7 11.5 %copy-start.3 = (s32[32,4]{0,1:T(4,128)S(1)}, s32[32,4]{0,1:T(4,128)}, u32[]{:S(2)}) copy-start(s32[32,4]{0,1:T(4,128)} %param.7) | copy-start | bytes 1540
  43.7 11.8 %collective-permute-start = (bf16[8,81,320]{2,0,1:T(8,128)(2,1)}, bf16[8,81,320]{2,0,1:T(8,128)(2,1)}, u32[]{:S(2)}, u32[]{:S(2)}) collective-permute-start(bf16[8,81,320]{2,0,1:T(8,128)(2,1)} %copy.18), channel_id=1, source_target_pairs={{0,16},{16,32},{32,48},{48,64},{64,80},{80,96},{96,112},{112,128},... | collective-permute-start | bytes 1244168 | tf_op jit(solution)/shard_map/ppermute | solution.py:22
  49.2 8.6 %collective-permute-start.1 = (bf16[8,81,320]{2,0,1:T(8,128)(2,1)}, bf16[8,81,320]{2,0,1:T(8,128)(2,1)}, u32[]{:S(2)}, u32[]{:S(2)}) collective-permute-start(bf16[8,81,320]{2,0,1:T(8,128)(2,1)} %copy.19), channel_id=1, source_target_pairs={{0,240},{16,0},{32,16},{48,32},{64,48},{80,64},{96,80},{112,96},{1... | collective-permute-start | bytes 1244168 | tf_op jit(solution)/shard_map/ppermute | solution.py:22
  50.1 9.7 %collective-permute-start.2 = (bf16[8,81,320]{2,0,1:T(8,128)(2,1)S(1)}, bf16[8,81,320]{2,0,1:T(8,128)(2,1)S(1)}, u32[]{:S(2)}, u32[]{:S(2)}) collective-permute-start(bf16[8,81,320]{2,0,1:T(8,128)(2,1)S(1)} %copy.20), channel_id=1, source_target_pairs={{0,1},{1,2},{2,3},{3,4},{4,5},{5,6},{6,7},{7,8},{8,9},{9,10},{10,1... | collective-permute-start | bytes 1244168 | tf_op jit(solution)/shard_map/ppermute | solution.py:28
  53.6 10.7 %collective-permute-start.3 = (bf16[8,81,320]{2,0,1:T(8,128)(2,1)S(1)}, bf16[8,81,320]{2,0,1:T(8,128)(2,1)S(1)}, u32[]{:S(2)}, u32[]{:S(2)}) collective-permute-start(bf16[8,81,320]{2,0,1:T(8,128)(2,1)S(1)} %copy.21), channel_id=1, source_target_pairs={{1,0},{2,1},{3,2},{4,3},{5,4},{6,5},{7,6},{8,7},{9,8},{10,9},{11,1... | collective-permute-start | bytes 1244168 | tf_op jit(solution)/shard_map/ppermute | solution.py:28
  96.5 10.9 %collective-permute-start.4 = (bf16[8,80]{1,0:T(8,128)(2,1)S(1)}, bf16[8,80]{1,0:T(8,128)(2,1)S(1)}, u32[]{:S(2)}, u32[]{:S(2)}) collective-permute-start(bf16[8,80]{1,0:T(8,128)(2,1)S(1)} %get-tuple-element.20), channel_id=1, source_target_pairs={{0,16},{16,32},{32,48},{48,64},{64,80},{80,96},{96,112},{112,128},... | collective-permute-start | bytes 3848 | tf_op jit(solution)/shard_map/ppermute | solution.py:22
  103.0 4.4 %collective-permute-start.5 = (bf16[8,80]{1,0:T(8,128)(2,1)S(1)}, bf16[8,80]{1,0:T(8,128)(2,1)S(1)}, u32[]{:S(2)}, u32[]{:S(2)}) collective-permute-start(bf16[8,80]{1,0:T(8,128)(2,1)S(1)} %get-tuple-element.19), channel_id=1, source_target_pairs={{0,240},{16,0},{32,16},{48,32},{64,48},{80,64},{96,80},{112,96},{1... | collective-permute-start | bytes 3848 | tf_op jit(solution)/shard_map/ppermute | solution.py:22
  103.1 4.4 %collective-permute-start.6 = (bf16[8,80]{1,0:T(8,128)(2,1)S(1)}, bf16[8,80]{1,0:T(8,128)(2,1)S(1)}, u32[]{:S(2)}, u32[]{:S(2)}) collective-permute-start(bf16[8,80]{1,0:T(8,128)(2,1)S(1)} %get-tuple-element.18), channel_id=1, source_target_pairs={{0,1},{1,2},{2,3},{3,4},{4,5},{5,6},{6,7},{7,8},{8,9},{9,10},{10,1... | collective-permute-start | bytes 3848 | tf_op jit(solution)/shard_map/ppermute | solution.py:28
  106.1 4.3 %collective-permute-start.7 = (bf16[8,80]{1,0:T(8,128)(2,1)S(1)}, bf16[8,80]{1,0:T(8,128)(2,1)S(1)}, u32[]{:S(2)}, u32[]{:S(2)}) collective-permute-start(bf16[8,80]{1,0:T(8,128)(2,1)S(1)} %get-tuple-element.17), channel_id=1, source_target_pairs={{1,0},{2,1},{3,2},{4,3},{5,4},{6,5},{7,6},{8,7},{9,8},{10,9},{11,1... | collective-permute-start | bytes 3848 | tf_op jit(solution)/shard_map/ppermute | solution.py:28
  112.8 6.4 %copy-start.1 = (bf16[8,64,80]{2,1,0:T(8,128)(2,1)S(1)}, bf16[8,64,80]{2,1,0:T(8,128)(2,1)}, u32[]{:S(2)}) copy-start(bf16[8,64,80]{2,1,0:T(8,128)(2,1)} %param.9) | copy-start | bytes 245764
where the time goes:
time: 278 us; the launch traced here: 277 us
  blocking collectives  155 us (56%)
  local copies, waits for them, and re-layouts  57 us (21%)
  matrix products  28.2 us (10%)
  starting transfers between devices  18.6 us (7%)
  waiting for transfers between devices  9.53 us (3%)
  other arithmetic  7.24 us (3%)
    psum x1, blocking collectives, per_device(): heights = lax.psum(local_heights, ('pitch', 'span')) * inverse_count  80.9 us
    psum x1, blocking collectives, per_device(): lax.psum(jnp.sum(remainder * remainder), ('pitch', 'span')) * inverse_count  74 us
    dot_general x4, matrix products, own_rows(): jnp.einsum('fij,fj->fi', block_rows, gathered, preferred_element_type=jnp...  25.6 us
    unnamed x15, local copies, waits for them, and re-layouts  21.2 us
    gather x1, local copies, waits for them, and re-layouts, per_device(): leading = blocks[flat_rows, :, :GSLOTS * BLOCK]  11.4 us
    ppermute x4, starting transfers between devices, shifted(): lax.ppermute(value, axis, [(i, (i + by) % devices) for i in range(devices)])  9.8 us
    ppermute x4, starting transfers between devices, shifted_2(): return lax.ppermute(value, axis, pairs)  8.75 us
    ppermute x4, waiting for transfers between devices, shifted_2(): return lax.ppermute(value, axis, pairs)  8.2 us
  transfers between devices with their start and end apart: 8, of which 4 were waited for; matrix products, arithmetic and copies ran while one was open for 2% of the time, Pallas kernels for 0%

commit v1 on v0

v1 whole, which is shorter than its diff:
```python
import functools

import jax
import jax.numpy as jnp
from jax import lax
from jax.experimental import pallas as pl
from jax.experimental.pallas import tpu as pltpu
from jax.sharding import PartitionSpec as P

BLOCK = 80
SLOTS = 11
GSLOTS = 4
F_DEV = 64
KRYLOV = 8
SWEEPS = 4
LIST = 8
LANES = 128
WIDTH = SLOTS * BLOCK
LEAD = 384
KTILES = ((0, 256), (256, 512), (512, 768), (768, 880))

center_value = 1.0
half_width = 0.5
epsilon = 1e-06

f32 = jnp.float32
bf16 = jnp.bfloat16
VMEM = pl.BlockSpec(memory_space=pltpu.VMEM)
SMEM = pl.BlockSpec(memory_space=pltpu.SMEM)
ANY = pl.BlockSpec(memory_space=pl.ANY)
PARAMS = pltpu.CompilerParams(vmem_limit_bytes=48 * 2**20)


def sweep_constants():
    stretch = center_value / half_width
    ratio_now = 1.0 / stretch
    factors = []
    for _ in range(SWEEPS - 1):
        ratio_next = 1.0 / (2.0 * stretch - ratio_now)
        factors.append((ratio_next * ratio_now, 2.0 * ratio_next / half_width))
        ratio_now = ratio_next
    return factors


def shifted(value, axis, by, wrap):
    devices = lax.axis_size(axis)
    pairs = [(i, (i + by) % devices) for i in range(devices) if wrap or 0 <= i + by < devices]
    return lax.ppermute(value, axis, pairs)


def exchange(outgoing):
    return [
        shifted(outgoing[0], "pitch", 1, True),
        shifted(outgoing[1], "pitch", -1, True),
        shifted(outgoing[2], "span", 1, False),
        shifted(outgoing[3], "span", -1, False),
    ]


def lane_ids():
    return lax.broadcasted_iota(jnp.int32, (BLOCK, LANES), 1)


def fill_columns(columns_ref, margin_ref, ids):
    ids[...] = jnp.full(ids.shape, LANES - 1, jnp.int32)
    ids[0:SLOTS, 0:F_DEV] = columns_ref[...]
    if margin_ref is not None:
        ids[0:GSLOTS, F_DEV : F_DEV + 4 * LIST] = margin_ref[...]


def fill_gathered(vector, ids, gathered):
    rows = lax.broadcasted_iota(jnp.int32, (LANES, LANES), 0)
    for slot in range(SLOTS):
        chosen = (rows == ids[slot : slot + 1, :]).astype(f32).astype(bf16)
        part = jnp.dot(vector, chosen, preferred_element_type=f32)
        gathered[slot * BLOCK : (slot + 1) * BLOCK, :] = part.astype(bf16)


def own_product(rows_ref, gathered, wait):
    lanes = lane_ids()
    total = jnp.zeros((BLOCK, LANES), f32)
    for index, (start, stop) in enumerate(KTILES):
        wait(index)
        rows = rows_ref[:, :, start:stop].reshape(F_DEV * BLOCK, stop - start)
        product = jnp.dot(rows, gathered[start:stop, :], preferred_element_type=f32)
        part = jnp.zeros((BLOCK, LANES), f32)
        for face in range(F_DEV):
            part = jnp.where(lanes == face, product[face * BLOCK : (face + 1) * BLOCK], part)
        total = total + part
    return total


def margin_product(row_refs, gathered):
    lanes = lane_ids()
    total = jnp.zeros((BLOCK, LANES), f32)
    for start, stop in ((0, 256), (256, LEAD)):
        part = jnp.zeros((BLOCK, LANES), f32)
        for index, ref in enumerate(row_refs):
            rows = ref[:, :, start:stop].reshape(LIST * BLOCK, stop - start)
            product = jnp.dot(rows, gathered[start:stop, :], preferred_element_type=f32)
            for face in range(LIST):
                lane = F_DEV + index * LIST + face
                part = jnp.where(lanes == lane, product[face * BLOCK : (face + 1) * BLOCK], part)
        total = total + part
    return total


def stage_rows(rows_hbm, rows_ref, sems):
    copies = []
    for index, (start, stop) in enumerate(KTILES):
        copy = pltpu.make_async_copy(
            rows_hbm.at[:, :, start:stop], rows_ref.at[:, :, start:stop], sems.at[index]
        )
        copy.start()
        copies.append(copy)
    return copies


def values_kernel(lists, latest, out0, out1, out2, out3, wide):
    wide[:, 0:BLOCK] = latest[...].astype(f32)
    wide[:, BLOCK:LANES] = jnp.zeros((F_DEV, LANES - BLOCK), f32)
    for index, out in enumerate((out0, out1, out2, out3)):
        for face in range(LIST):
            out[face : face + 1, :] = wide[pl.ds(lists[index, face], 1), :]


def rows_kernel(lists, rows, out0, out1, out2, out3, sem):
    copies = []
    for index, out in enumerate((out0, out1, out2, out3)):
        for face in range(LIST):
            copy = pltpu.make_async_copy(
                rows.at[lists[index, face], :, pl.ds(0, LEAD)], out.at[face], sem.at[index * LIST + face]
            )
            copy.start()
            copies.append(copy)
    for copy in copies:
        copy.wait()


def first_kernel(rows_hbm, columns, latest, g0, g1, g2, g3, residual_out, applied_out, rows, sems, wide, ids, gathered):
    copies = stage_rows(rows_hbm, rows, sems)
    fill_columns(columns, None, ids)
    wide[...] = jnp.zeros((LANES, LANES), f32)
    wide[0:F_DEV, 0:BLOCK] = latest[...].astype(f32)
    for index, ghost in enumerate((g0, g1, g2, g3)):
        start = F_DEV + index * LIST
        wide[start : start + LIST, :] = ghost[...]
    residual = wide[...].T[0:BLOCK]
    residual_out[...] = residual
    fill_gathered((residual / center_value).astype(bf16), ids, gathered)
    applied_out[...] = own_product(rows, gathered, lambda index: copies[index].wait())


def sweeps_kernel(
    rows_hbm, columns, margin_columns, lists, residual_in, applied_in, m0, m1, m2, m3,
    precond_out, out0, out1, out2, out3, rows, sems, wide, ids, gathered,
):
    copies = stage_rows(rows_hbm, rows, sems)
    fill_columns(columns, margin_columns, ids)
    factors = sweep_constants()
    margins = (m0, m1, m2, m3)
    residual = residual_in[...]
    direction = residual / center_value
    solution = direction
    for sweep in range(SWEEPS - 1):
        fill_gathered(direction.astype(bf16), ids, gathered)
        if sweep == 0:
            applied = applied_in[...]
        elif sweep == 1:
            applied = own_product(rows, gathered, lambda index: copies[index].wait())
        else:
            applied = own_product(rows, gathered, lambda index: None)
        if sweep < SWEEPS - 2:
            applied = applied + margin_product(margins, gathered)
        residual = residual - applied
        keep_factor, push_factor = factors[sweep]
        direction = keep_factor * direction + push_factor * residual
        solution = solution + direction
    own = jnp.where(lane_ids() < F_DEV, solution, 0.0).astype(bf16)
    precond_out[...] = own
    wide[0:BLOCK, :] = own.astype(f32)
    wide[BLOCK:LANES, :] = jnp.zeros((LANES - BLOCK, LANES), f32)
    wide[...] = wide[...].T
    for index, out in enumerate((out0, out1, out2, out3)):
        for face in range(LIST):
            out[face : face + 1, :] = wide[pl.ds(lists[index, face], 1), :]


PAIRS = [(a, b) for a in range(KRYLOV) for b in range(a, KRYLOV)]
SUMS = KRYLOV + 1 + len(PAIRS)


def image_kernel(rows_hbm, columns, precond, g0, g1, g2, g3, basis, image_out, sums_out, rows, sems, wide, ids, gathered, sums):
    copies = stage_rows(rows_hbm, rows, sems)
    fill_columns(columns, None, ids)
    wide[...] = jnp.zeros((LANES, LANES), f32)
    for index, ghost in enumerate((g0, g1, g2, g3)):
        start = F_DEV + index * LIST
        wide[start : start + LIST, :] = ghost[...]
    vector = precond[...] + wide[...].T[0:BLOCK].astype(bf16)
    fill_gathered(vector, ids, gathered)
    sums[...] = jnp.zeros((LANES, LANES), f32)
    spread = [basis[j].astype(f32) for j in range(KRYLOV)]
    for index, (a, b) in enumerate(PAIRS):
        row = KRYLOV + 1 + index
        sums[row : row + 1, 0:BLOCK] = jnp.sum(spread[a] * spread[b], axis=0, keepdims=True)
    product = own_product(rows, gathered, lambda index: copies[index].wait())
    wide[0:BLOCK, :] = product
    wide[BLOCK:LANES, :] = jnp.zeros((LANES - BLOCK, LANES), f32)
    image = wide[...].T[0:F_DEV, 0:BLOCK]
    image_out[...] = image
    for j in range(KRYLOV):
        sums[j : j + 1, 0:BLOCK] = jnp.sum(spread[j] * image, axis=0, keepdims=True)
    sums[KRYLOV : KRYLOV + 1, 0:BLOCK] = jnp.sum(image * image, axis=0, keepdims=True)
    totals = jnp.sum(sums[...], axis=1, keepdims=True)
    row = jnp.broadcast_to(totals, (LANES, LANES)).T[0:1]
    sums_out[...] = jnp.broadcast_to(row, sums_out.shape)


def last_kernel(inverse_count, image, basis, sums, vector_out, projections_out):
    totals = jnp.sum(sums[...], axis=0, keepdims=True) * inverse_count
    entry = lambda index: totals[:, index : index + 1]
    heights = [entry(j) for j in range(KRYLOV)]
    squares = entry(KRYLOV)
    for index, (a, b) in enumerate(PAIRS):
        term = heights[a] * heights[b] * entry(KRYLOV + 1 + index)
        squares = squares + (term if a == b else 2.0 * term)
    for j in range(KRYLOV):
        squares = squares - 2.0 * heights[j] * heights[j]
    length = jnp.sqrt(squares + epsilon)
    remainder = image[...]
    for j in range(KRYLOV):
        remainder = remainder - heights[j] * basis[j].astype(f32)
    vector_out[...] = (remainder / length).astype(bf16)
    lanes = lax.broadcasted_iota(jnp.int32, (1, LANES), 1)
    projections_out[...] = jnp.where(lanes == KRYLOV, length, totals)


def shape(dims, dtype):
    return jax.ShapeDtypeStruct(dims, dtype)


def per_device(blocks, columns, margin_columns, send_lists, basis):
    devices = lax.axis_size("pitch") * lax.axis_size("span")
    latest = basis[KRYLOV - 1]
    columns_t = columns.T
    margin_t = margin_columns.T
    row_scratch = pltpu.VMEM((F_DEV, BLOCK, WIDTH), bf16)
    row_sems = pltpu.SemaphoreType.DMA((len(KTILES),))
    square = pltpu.VMEM((LANES, LANES), f32)
    ids = pltpu.VMEM((16, LANES), jnp.int32)
    gathered = pltpu.VMEM((WIDTH, LANES), bf16)

    values = pl.pallas_call(
        values_kernel,
        out_shape=[shape((LIST, LANES), f32)] * 4,
        in_specs=[SMEM, VMEM],
        out_specs=[VMEM] * 4,
        scratch_shapes=[pltpu.VMEM((F_DEV, LANES), f32)],
        name="pack_values",
    )(send_lists, latest)
    ghosts = exchange(values)
    leading = pl.pallas_call(
        rows_kernel,
        out_shape=[shape((LIST, BLOCK, LEAD), bf16)] * 4,
        in_specs=[SMEM, ANY],
        out_specs=[ANY] * 4,
        scratch_shapes=[pltpu.SemaphoreType.DMA((4 * LIST,))],
        name="pack_rows",
    )(send_lists, blocks)
    margins = exchange(leading)
    residual, applied = pl.pallas_call(
        first_kernel,
        out_shape=[shape((BLOCK, LANES), f32)] * 2,
        in_specs=[ANY] + [VMEM] * 6,
        out_specs=[VMEM] * 2,
        scratch_shapes=[row_scratch, row_sems, square, ids, gathered],
        compiler_params=PARAMS,
        name="first_product",
    )(blocks, columns_t, latest, *ghosts)
    precond, *values = pl.pallas_call(
        sweeps_kernel,
        out_shape=[shape((BLOCK, LANES), bf16)] + [shape((LIST, LANES), f32)] * 4,
        in_specs=[ANY, VMEM, VMEM, SMEM] + [VMEM] * 6,
        out_specs=[VMEM] * 5,
        scratch_shapes=[row_scratch, row_sems, square, ids, gathered],
        compiler_params=PARAMS,
        name="sweeps",
    )(blocks, columns_t, margin_t, send_lists, residual, applied, *margins)
    ghosts = exchange(values)
    image, sums = pl.pallas_call(
        image_kernel,
        out_shape=[shape((F_DEV, BLOCK), f32), shape((devices, LANES), f32)],
        in_specs=[ANY] + [VMEM] * 7,
        out_specs=[VMEM] * 2,
        scratch_shapes=[row_scratch, row_sems, square, ids, gathered, square],
        compiler_params=PARAMS,
        name="image",
    )(blocks, columns_t, precond, *ghosts, basis)
    sums = lax.all_to_all(sums.reshape(devices, 1, LANES), ("pitch", "span"), 0, 0)
    new_vector, projections = pl.pallas_call(
        functools.partial(last_kernel, 1.0 / (devices * F_DEV * BLOCK)),
        out_shape=[shape((F_DEV, BLOCK), bf16), shape((1, LANES), f32)],
        in_specs=[VMEM] * 3,
        out_specs=[VMEM] * 2,
        name="new_vector",
    )(image, basis, sums.reshape(devices, LANES))
    return (new_vector, projections[0, 0 : KRYLOV + 1])


def solution(mesh):
    return jax.shard_map(
        per_device,
        mesh=mesh,
        in_specs=(
            P(("pitch", "span"), None, None),
            P(("pitch", "span"), None),
            P(("pitch", "span"), None),
            P(("pitch", "span"), None),
            P(None, ("pitch", "span"), None),
        ),
        out_specs=(P(("pitch", "span"), None), P()),
        check_vma=False,
    )
```

time: 278 us -> 168 us (0.60)
  blocking collectives: 155 us -> 34.7 us
  Pallas kernels: 0 us -> 91.9 us
  local copies, waits for them, and re-layouts: 57 us -> 2.53 us
  matrix products: 28.2 us -> 0 us
  starting transfers between devices: 18.6 us -> 26.1 us
  other arithmetic: 7.24 us -> 0 us
    psum x2 -> x0, blocking collectives: 155 us -> none  [the longest x1 80.9 us: per_device(): heights = lax.psum(local_heights, ('pitch', 'span')) * inverse_count]
    pallas_call x0 -> x6, Pallas kernels: none -> 91.9 us  [the longest x1 61.8 us: per_device(): pl.pallas_call(rows_kernel, out_shape=[shape((LIST, BLOCK, LEAD), bf16)]...]
    all_to_all x0 -> x1, blocking collectives: none -> 34.7 us  [per_device(): lax.all_to_all(sums.reshape(devices, 1, LANES), ('pitch', 'span'), 0, 0)]
    dot_general x8 -> x0, matrix products: 28.2 us -> none  [the longest x4 25.6 us: own_rows(): jnp.einsum('fij,fj->fi', block_rows, gathered, preferred_element_type=jnp...]
    gather x10 -> x0, local copies, waits for them, and re-layouts: 22.9 us -> none  [the longest x1 11.4 us: per_device(): leading = blocks[flat_rows, :, :GSLOTS * BLOCK]]
    unnamed x15 -> x12, local copies, waits for them, and re-layouts: 21.2 us -> 0.74 us
    ppermute x8 -> x12, starting transfers between devices: 18.6 us -> 26.1 us  [shifted(): return lax.ppermute(value, axis, pairs)]
    slice x6 -> x0, local copies, waits for them, and re-layouts: 6.52 us -> none  [the longest x2 5.08 us: forward_rows(): received.append(shifted(outgoing[list_index], 'pitch', offset))]
  transfers between devices with their start and end apart: 8 -> 12, of which waited for: 4 -> 5; matrix products, arithmetic and copies ran while one was open for 2% -> 0% of each run, Pallas kernels for 0% -> 5%
where the time goes in v1:
time: 168 us
  Pallas kernels  91.9 us (55%)
  blocking collectives  34.7 us (21%)
  starting transfers between devices  26.1 us (16%)
  waiting for transfers between devices  11.7 us (7%)
  local copies, waits for them, and re-layouts  2.53 us (2%)
    pallas_call x1, Pallas kernels, per_device(): pl.pallas_call(rows_kernel, out_shape=[shape((LIST, BLOCK, LEAD), bf16)]...  61.8 us
    all_to_all x1, blocking collectives, per_device(): lax.all_to_all(sums.reshape(devices, 1, LANES), ('pitch', 'span'), 0, 0)  34.7 us
    ppermute x12, starting transfers between devices, shifted(): return lax.ppermute(value, axis, pairs)  26.1 us
    pallas_call x1, Pallas kernels, per_device(): pl.pallas_call(sweeps_kernel, out_shape=[shape((BLOCK, LANES), bf16)] + [...  12.6 us
    ppermute x12, waiting for transfers between devices, shifted(): return lax.ppermute(value, axis, pairs)  11.7 us
    pallas_call x1, Pallas kernels, per_device(): pl.pallas_call(image_kernel, out_shape=[shape((F_DEV, BLOCK), f32), shape...  7.32 us
    pallas_call x1, Pallas kernels, per_device(): pl.pallas_call(first_kernel, out_shape=[shape((BLOCK, LANES), f32)] * 2,...  6.91 us
  transfers between devices with their start and end apart: 12, of which 5 were waited for; matrix products, arithmetic and copies ran while one was open for 0% of the time, Pallas kernels for 5%

profile of v1, /device:TPU:1, one launch (start us, length us, event | category | flops | bytes accessed | tf_op | source)
XLA Modules:
  0.0 167.7 jit_solution(9422333837864005261)
XLA Ops:
  0.6 0.0 copy-start.4
  0.6 0.0 copy-start
  0.7 0.0 copy-start.2
  0.7 0.0 copy-start.5
  0.7 61.8 %pack_rows.1 = (bf16[8,80,384]{2,1,0:T(8,128)(2,1)}, bf16[8,80,384]{2,1,0:T(8,128)(2,1)}, bf16[8,80,384]{2,1,0:T(8,128)(2,1)}, bf16[8,80,384]{2,1,0:T(8,128)(2,1)}) custom-call(s32[4,8]{1,0:T(4,128)} %lists.5, bf16[64,80,880]{2,1,0:T(8,128)(2,1)} %rows_hbm.5), custom_call_target="tpu_custom_call" | custom-call | tf_op jit(solution)/shard_map/pack_rows/pallas_call | solution.py:263
  62.5 3.0 %collective-permute-start.4 = (bf16[8,80,384]{2,1,0:T(8,128)(2,1)}, bf16[8,80,384]{2,1,0:T(8,128)(2,1)S(1)}, u32[]{:S(2)}, u32[]{:S(2)}) collective-permute-start(bf16[8,80,384]{2,1,0:T(8,128)(2,1)} %get-tuple-element.27), channel_id=1, source_target_pairs={{0,16},{16,32},{32,48},{48,64},{64,80},{80,96},{96,112},{112,128},... | collective-permute-start | bytes 1474568 | tf_op jit(solution)/shard_map/ppermute | solution.py:48
  65.5 0.2 collective-permute-start.5
  65.7 2.9 %collective-permute-start.6 = (bf16[8,80,384]{2,1,0:T(8,128)(2,1)}, bf16[8,80,384]{2,1,0:T(8,128)(2,1)S(1)}, u32[]{:S(2)}, u32[]{:S(2)}) collective-permute-start(bf16[8,80,384]{2,1,0:T(8,128)(2,1)} %get-tuple-element.29), channel_id=1, source_target_pairs={{0,1},{1,2},{2,3},{3,4},{4,5},{5,6},{6,7},{7,8},{8,9},{9,10},{10,1... | collective-permute-start | bytes 1474568 | tf_op jit(solution)/shard_map/ppermute | solution.py:48
  68.6 1.3 collective-permute-start.7
  69.9 0.0 copy-done
  70.0 0.6 slice_bitcast_fusion.latest
  70.6 1.3 pack_values.1
  71.9 2.0 %collective-permute-start = (f32[8,128]{1,0:T(8,128)}, f32[8,128]{1,0:T(8,128)S(1)}, u32[]{:S(2)}, u32[]{:S(2)}) collective-permute-start(f32[8,128]{1,0:T(8,128)} %get-tuple-element.21), channel_id=1, source_target_pairs={{0,16},{16,32},{32,48},{48,64},{64,80},{80,96},{96,112},{112,128},... | collective-permute-start | bytes 12296 | tf_op jit(solution)/shard_map/ppermute | solution.py:48
  73.9 2.9 %collective-permute-done.g0 = f32[8,128]{1,0:T(8,128)S(1)} collective-permute-done((f32[8,128]{1,0:T(8,128)}, f32[8,128]{1,0:T(8,128)S(1)}, u32[]{:S(2)}, u32[]{:S(2)}) %collective-permute-start) | collective-permute-done | bytes 4128 | tf_op jit(solution)/shard_map/ppermute | solution.py:48
  76.9 3.6 %collective-permute-start.1 = (f32[8,128]{1,0:T(8,128)}, f32[8,128]{1,0:T(8,128)S(1)}, u32[]{:S(2)}, u32[]{:S(2)}) collective-permute-start(f32[8,128]{1,0:T(8,128)} %get-tuple-element.22), channel_id=1, source_target_pairs={{0,240},{16,0},{32,16},{48,32},{64,48},{80,64},{96,80},{112,96},{1... | collective-permute-start | bytes 12296 | tf_op jit(solution)/shard_map/ppermute | solution.py:48
  80.4 1.0 collective-permute-done.1.g1
  81.5 4.3 %collective-permute-start.2 = (f32[8,128]{1,0:T(8,128)}, f32[8,128]{1,0:T(8,128)S(1)}, u32[]{:S(2)}, u32[]{:S(2)}) collective-permute-start(f32[8,128]{1,0:T(8,128)} %get-tuple-element.23), channel_id=1, source_target_pairs={{0,1},{1,2},{2,3},{3,4},{4,5},{5,6},{6,7},{7,8},{8,9},{9,10},{10,1... | collective-permute-start | bytes 12296 | tf_op jit(solution)/shard_map/ppermute | solution.py:48
  85.7 0.9 collective-permute-done.2.g2
  86.7 1.3 collective-permute-start.3
  88.0 3.5 %collective-permute-done.3.g3 = f32[8,128]{1,0:T(8,128)S(1)} collective-permute-done((f32[8,128]{1,0:T(8,128)}, f32[8,128]{1,0:T(8,128)S(1)}, u32[]{:S(2)}, u32[]{:S(2)}) %collective-permute-start.3) | collective-permute-done | bytes 4128 | tf_op jit(solution)/shard_map/ppermute | solution.py:48
  91.5 0.0 copy-done.2
  91.5 0.0 copy-start.1
  91.5 0.7 copy-done.1
  92.2 6.9 %first_product.1 = (f32[80,128]{1,0:T(8,128)S(1)}, f32[80,128]{1,0:T(8,128)S(1)}) custom-call(bf16[64,80,880]{2,1,0:T(8,128)(2,1)} %rows_hbm.5, s32[11,64]{1,0:T(8,128)S(1)} %bitcast.11, bf16[64,80]{1,0:T(8,128)(2,1)S(1)} %copy-done.1, f32[8,128]{1,0:T(8,128)S(1)} %collective-permute-done.g0, f32[8,128]{1,0:T(8,128)S(1)} %collective-permute-done.1.g1, ...), custom_call_target="tpu_custom_call" | custom-call | tf_op jit(solution)/shard_map/first_product/pallas_call | solution.py:272
  99.1 0.0 collective-permute-done.4.m0
  99.1 0.0 collective-permute-done.5.m1
  99.1 0.0 collective-permute-done.6.m2
  99.2 0.0 collective-permute-done.7.m3
  99.2 0.0 copy-done.4
  99.2 0.0 copy-done.5
  99.2 12.6 %sweeps.1 = (bf16[80,128]{1,0:T(8,128)(2,1)S(1)}, f32[8,128]{1,0:T(8,128)S(1)}, f32[8,128]{1,0:T(8,128)S(1)}, f32[8,128]{1,0:T(8,128)S(1)}, f32[8,128]{1,0:T(8,128)S(1)}) custom-call(bf16[64,80,880]{2,1,0:T(8,128)(2,1)} %rows_hbm.5, s32[11,64]{1,0:T(8,128)S(1)} %bitcast.12, s32[4,32]{1,0:T(4,128)S(1)} %bitcast.14, s32[4,8]{1,0:T(4,128)S(1)} %copy-done.4, ...), custom_call_target="tpu_custom_call" | custom-call | tf_op jit(solution)/shard_map/sweeps/pallas_call | solution.py:281
  111.8 0.7 collective-permute-start.8
  112.5 1.9 %collective-permute-start.9 = (f32[8,128]{1,0:T(8,128)S(1)}, f32[8,128]{1,0:T(8,128)S(1)}, u32[]{:S(2)}, u32[]{:S(2)}) collective-permute-start(f32[8,128]{1,0:T(8,128)S(1)} %get-tuple-element.33), channel_id=1, source_target_pairs={{0,240},{16,0},{32,16},{48,32},{64,48},{80,64},{96,80},{112,96},{1... | collective-permute-start | bytes 12296 | tf_op jit(solution)/shard_map/ppermute | solution.py:48
  114.3 3.6 %collective-permute-start.10 = (f32[8,128]{1,0:T(8,128)S(1)}, f32[8,128]{1,0:T(8,128)S(1)}, u32[]{:S(2)}, u32[]{:S(2)}) collective-permute-start(f32[8,128]{1,0:T(8,128)S(1)} %get-tuple-element.34), channel_id=1, source_target_pairs={{0,1},{1,2},{2,3},{3,4},{4,5},{5,6},{6,7},{7,8},{8,9},{9,10},{10,1... | collective-permute-start | bytes 12296 | tf_op jit(solution)/shard_map/ppermute | solution.py:48
  118.0 1.3 collective-permute-start.11
  119.3 0.0 collective-permute-done.8.g0
  119.3 0.0 collective-permute-done.9.g1
  119.3 0.0 collective-permute-done.10.g2
  119.3 3.3 %collective-permute-done.11.g3 = f32[8,128]{1,0:T(8,128)S(1)} collective-permute-done((f32[8,128]{1,0:T(8,128)S(1)}, f32[8,128]{1,0:T(8,128)S(1)}, u32[]{:S(2)}, u32[]{:S(2)}) %collective-permute-start.11) | collective-permute-done | bytes 4128 | tf_op jit(solution)/shard_map/ppermute | solution.py:48
  122.6 7.3 %image.1 = (f32[64,80]{1,0:T(8,128)S(1)}, f32[256,128]{1,0:T(8,128)S(1)}) custom-call(bf16[64,80,880]{2,1,0:T(8,128)(2,1)} %rows_hbm.5, s32[11,64]{1,0:T(8,128)S(1)} %bitcast.13, bf16[80,128]{1,0:T(8,128)(2,1)S(1)} %get-tuple-element.31.precond, f32[8,128]{1,0:T(8,128)S(1)} %collective-permute-done.8.g0, f32[8,128]{1,0:T(8,128)S(1)} %collective-permute-done.9.g1, ...), custom_call_target="tpu_custom_call" | custom-call | tf_op jit(solution)/shard_map/image/pallas_call | solution.py:291
  129.9 0.0 copy-start.3
  129.9 34.7 %all_to_all.5 = f32[256,1,128]{2,1,0:T(1,128)} all-to-all(f32[256,1,128]{2,1,0:T(1,128)S(1)} %bitcast.10), channel_id=1, replica_groups=mesh['pitch'=16,'span'=16] {'pitch','span'}, dimensions={0} | all-to-all | bytes 262144 | tf_op jit(solution)/shard_map/all_to_all | solution.py:300
  164.6 0.0 copy-done.3
  164.6 1.9 %new_vector.1 = (bf16[64,80]{1,0:T(8,128)(2,1)}, f32[1,128]{1,0:T(1,128)}) custom-call(f32[64,80]{1,0:T(8,128)} %copy-done.3, bf16[8,64,80]{2,1,0:T(8,128)(2,1)} %basis.3, f32[256,128]{1,0:T(8,128)} %bitcast.15), custom_call_target="tpu_custom_call" | custom-call | tf_op jit(solution)/shard_map/new_vector/pallas_call | solution.py:301
  166.5 1.2 slice_bitcast_fusion.1
Async XLA Ops:
  0.6 98.5 %copy-start.4 = (s32[4,8]{1,0:T(4,128)S(1)}, s32[4,8]{1,0:T(4,128)}, u32[]{:S(2)}) copy-start(s32[4,8]{1,0:T(4,128)} %lists.5) | copy-start | bytes 388
  0.6 69.3 %copy-start = (bf16[8,64,80]{2,1,0:T(8,128)(2,1)S(1)}, bf16[8,64,80]{2,1,0:T(8,128)(2,1)}, u32[]{:S(2)}) copy-start(bf16[8,64,80]{2,1,0:T(8,128)(2,1)} %basis.3) | copy-start | bytes 245764
  0.7 90.8 %copy-start.2 = (s32[64,11]{0,1:T(8,128)S(1)}, s32[64,11]{0,1:T(8,128)}, u32[]{:S(2)}) copy-start(s32[64,11]{0,1:T(8,128)} %param.6) | copy-start | bytes 8452
  0.7 98.5 %copy-start.5 = (s32[32,4]{0,1:T(4,128)S(1)}, s32[32,4]{0,1:T(4,128)}, u32[]{:S(2)}) copy-start(s32[32,4]{0,1:T(4,128)} %param.7) | copy-start | bytes 1540
  62.5 36.7 %collective-permute-start.4 = (bf16[8,80,384]{2,1,0:T(8,128)(2,1)}, bf16[8,80,384]{2,1,0:T(8,128)(2,1)S(1)}, u32[]{:S(2)}, u32[]{:S(2)}) collective-permute-start(bf16[8,80,384]{2,1,0:T(8,128)(2,1)} %get-tuple-element.27), channel_id=1, source_target_pairs={{0,16},{16,32},{32,48},{48,64},{64,80},{80,96},{96,112},{112,128},... | collective-permute-start | bytes 1474568 | tf_op jit(solution)/shard_map/ppermute | solution.py:48
  65.5 33.6 %collective-permute-start.5 = (bf16[8,80,384]{2,1,0:T(8,128)(2,1)}, bf16[8,80,384]{2,1,0:T(8,128)(2,1)S(1)}, u32[]{:S(2)}, u32[]{:S(2)}) collective-permute-start(bf16[8,80,384]{2,1,0:T(8,128)(2,1)} %get-tuple-element.28), channel_id=1, source_target_pairs={{0,240},{16,0},{32,16},{48,32},{64,48},{80,64},{96,80},{112,96},{1... | collective-permute-start | bytes 1474568 | tf_op jit(solution)/shard_map/ppermute | solution.py:48
  65.7 33.4 %collective-permute-start.6 = (bf16[8,80,384]{2,1,0:T(8,128)(2,1)}, bf16[8,80,384]{2,1,0:T(8,128)(2,1)S(1)}, u32[]{:S(2)}, u32[]{:S(2)}) collective-permute-start(bf16[8,80,384]{2,1,0:T(8,128)(2,1)} %get-tuple-element.29), channel_id=1, source_target_pairs={{0,1},{1,2},{2,3},{3,4},{4,5},{5,6},{6,7},{7,8},{8,9},{9,10},{10,1... | collective-permute-start | bytes 1474568 | tf_op jit(solution)/shard_map/ppermute | solution.py:48
  68.6 30.5 %collective-permute-start.7 = (bf16[8,80,384]{2,1,0:T(8,128)(2,1)}, bf16[8,80,384]{2,1,0:T(8,128)(2,1)S(1)}, u32[]{:S(2)}, u32[]{:S(2)}) collective-permute-start(bf16[8,80,384]{2,1,0:T(8,128)(2,1)} %get-tuple-element.30), channel_id=1, source_target_pairs={{1,0},{2,1},{3,2},{4,3},{5,4},{6,5},{7,6},{8,7},{9,8},{10,9},{11,1... | collective-permute-start | bytes 1474568 | tf_op jit(solution)/shard_map/ppermute | solution.py:48
  71.9 4.9 %collective-permute-start = (f32[8,128]{1,0:T(8,128)}, f32[8,128]{1,0:T(8,128)S(1)}, u32[]{:S(2)}, u32[]{:S(2)}) collective-permute-start(f32[8,128]{1,0:T(8,128)} %get-tuple-element.21), channel_id=1, source_target_pairs={{0,16},{16,32},{32,48},{48,64},{64,80},{80,96},{96,112},{112,128},... | collective-permute-start | bytes 12296 | tf_op jit(solution)/shard_map/ppermute | solution.py:48
  76.9 4.6 %collective-permute-start.1 = (f32[8,128]{1,0:T(8,128)}, f32[8,128]{1,0:T(8,128)S(1)}, u32[]{:S(2)}, u32[]{:S(2)}) collective-permute-start(f32[8,128]{1,0:T(8,128)} %get-tuple-element.22), channel_id=1, source_target_pairs={{0,240},{16,0},{32,16},{48,32},{64,48},{80,64},{96,80},{112,96},{1... | collective-permute-start | bytes 12296 | tf_op jit(solution)/shard_map/ppermute | solution.py:48
  81.5 5.2 %collective-permute-start.2 = (f32[8,128]{1,0:T(8,128)}, f32[8,128]{1,0:T(8,128)S(1)}, u32[]{:S(2)}, u32[]{:S(2)}) collective-permute-start(f32[8,128]{1,0:T(8,128)} %get-tuple-element.23), channel_id=1, source_target_pairs={{0,1},{1,2},{2,3},{3,4},{4,5},{5,6},{6,7},{7,8},{8,9},{9,10},{10,1... | collective-permute-start | bytes 12296 | tf_op jit(solution)/shard_map/ppermute | solution.py:48
  86.7 4.8 %collective-permute-start.3 = (f32[8,128]{1,0:T(8,128)}, f32[8,128]{1,0:T(8,128)S(1)}, u32[]{:S(2)}, u32[]{:S(2)}) collective-permute-start(f32[8,128]{1,0:T(8,128)} %get-tuple-element.24), channel_id=1, source_target_pairs={{1,0},{2,1},{3,2},{4,3},{5,4},{6,5},{7,6},{8,7},{9,8},{10,9},{11,1... | collective-permute-start | bytes 12296 | tf_op jit(solution)/shard_map/ppermute | solution.py:48
  91.5 0.7 copy-start.1
  111.8 7.5 %collective-permute-start.8 = (f32[8,128]{1,0:T(8,128)S(1)}, f32[8,128]{1,0:T(8,128)S(1)}, u32[]{:S(2)}, u32[]{:S(2)}) collective-permute-start(f32[8,128]{1,0:T(8,128)S(1)} %get-tuple-element.32), channel_id=1, source_target_pairs={{0,16},{16,32},{32,48},{48,64},{64,80},{80,96},{96,112},{112,128},... | collective-permute-start | bytes 12296 | tf_op jit(solution)/shard_map/ppermute | solution.py:48
  112.5 6.8 %collective-permute-start.9 = (f32[8,128]{1,0:T(8,128)S(1)}, f32[8,128]{1,0:T(8,128)S(1)}, u32[]{:S(2)}, u32[]{:S(2)}) collective-permute-start(f32[8,128]{1,0:T(8,128)S(1)} %get-tuple-element.33), channel_id=1, source_target_pairs={{0,240},{16,0},{32,16},{48,32},{64,48},{80,64},{96,80},{112,96},{1... | collective-permute-start | bytes 12296 | tf_op jit(solution)/shard_map/ppermute | solution.py:48
  114.3 4.9 %collective-permute-start.10 = (f32[8,128]{1,0:T(8,128)S(1)}, f32[8,128]{1,0:T(8,128)S(1)}, u32[]{:S(2)}, u32[]{:S(2)}) collective-permute-start(f32[8,128]{1,0:T(8,128)S(1)} %get-tuple-element.34), channel_id=1, source_target_pairs={{0,1},{1,2},{2,3},{3,4},{4,5},{5,6},{6,7},{7,8},{8,9},{9,10},{10,1... | collective-permute-start | bytes 12296 | tf_op jit(solution)/shard_map/ppermute | solution.py:48
  118.0 4.6 %collective-permute-start.11 = (f32[8,128]{1,0:T(8,128)S(1)}, f32[8,128]{1,0:T(8,128)S(1)}, u32[]{:S(2)}, u32[]{:S(2)}) collective-permute-start(f32[8,128]{1,0:T(8,128)S(1)} %get-tuple-element.35), channel_id=1, source_target_pairs={{1,0},{2,1},{3,2},{4,3},{5,4},{6,5},{7,6},{8,7},{9,8},{10,9},{11,1... | collective-permute-start | bytes 12296 | tf_op jit(solution)/shard_map/ppermute | solution.py:48
  129.9 34.7 %copy-start.3 = (f32[64,80]{1,0:T(8,128)}, f32[64,80]{1,0:T(8,128)S(1)}, u32[]{:S(2)}) copy-start(f32[64,80]{1,0:T(8,128)S(1)} %get-tuple-element.36.image) | copy-start | bytes 61444

commit v2 on v1

v2 whole, which is shorter than its diff:
```python
import functools

import jax
import jax.numpy as jnp
from jax import lax
from jax.experimental import pallas as pl
from jax.experimental.pallas import tpu as pltpu
from jax.sharding import PartitionSpec as P

BLOCK = 80
SLOTS = 11
GSLOTS = 4
F_DEV = 64
KRYLOV = 8
SWEEPS = 4
LIST = 8
LANES = 128
WIDTH = SLOTS * BLOCK
MESSAGE = 208
KTILES = ((0, 256), (256, 512), (512, 768), (768, 880))

center_value = 1.0
half_width = 0.5
epsilon = 1e-06

f32 = jnp.float32
bf16 = jnp.bfloat16
VMEM = pl.BlockSpec(memory_space=pltpu.VMEM)
SMEM = pl.BlockSpec(memory_space=pltpu.SMEM)
ANY = pl.BlockSpec(memory_space=pl.ANY)
PARAMS = pltpu.CompilerParams(vmem_limit_bytes=32 * 2**20)


def sweep_constants():
    stretch = center_value / half_width
    ratio_now = 1.0 / stretch
    factors = []
    for _ in range(SWEEPS - 1):
        ratio_next = 1.0 / (2.0 * stretch - ratio_now)
        factors.append((ratio_next * ratio_now, 2.0 * ratio_next / half_width))
        ratio_now = ratio_next
    return factors


def positions():
    return lax.axis_index("pitch") % 2, lax.axis_index("span") % 2


def sent_lists():
    pitch_odd, span_odd = positions()
    return pitch_odd, 1 - pitch_odd, 2 + span_odd, 3 - span_odd


def received_groups():
    pitch_odd, span_odd = positions()
    return 1 - pitch_odd, pitch_odd, 3 - span_odd, 2 + span_odd


def exchange(outgoing):
    pitch, span = lax.axis_size("pitch"), lax.axis_size("span")
    received = []
    for index, value in enumerate(outgoing):
        axis, devices, wrap = ("pitch", pitch, True) if index < 2 else ("span", span, False)
        first = index % 2
        pairs = []
        for low in range(first, devices, 2):
            high = low + 1
            if high < devices or wrap:
                pairs += [(low, high % devices), (high % devices, low)]
        received.append(lax.ppermute(value, axis, pairs))
    return received


def lane_ids():
    return lax.broadcasted_iota(jnp.int32, (BLOCK, LANES), 1)


def fill_columns(columns_ref, margin_ref, ids):
    ids[...] = jnp.full(ids.shape, LANES - 1, jnp.int32)
    ids[0:SLOTS, 0:F_DEV] = columns_ref[...]
    if margin_ref is not None:
        ids[0:GSLOTS, F_DEV : F_DEV + 4 * LIST] = margin_ref[...]


def fill_gathered(vector, ids, gathered):
    rows = lax.broadcasted_iota(jnp.int32, (LANES, LANES), 0)
    for slot in range(SLOTS):
        chosen = (rows == ids[slot : slot + 1, :]).astype(f32).astype(bf16)
        part = jnp.dot(vector, chosen, preferred_element_type=f32)
        gathered[slot * BLOCK : (slot + 1) * BLOCK, :] = part.astype(bf16)


def own_product(rows_ref, gathered):
    lanes = lane_ids()
    total = jnp.zeros((BLOCK, LANES), f32)
    for start, stop in KTILES:
        rows = rows_ref[:, :, start:stop].reshape(F_DEV * BLOCK, stop - start)
        product = jnp.dot(rows, gathered[start:stop, :], preferred_element_type=f32)
        part = jnp.zeros((BLOCK, LANES), f32)
        for face in range(F_DEV):
            part = jnp.where(lanes == face, product[face * BLOCK : (face + 1) * BLOCK], part)
        total = total + part
    return total


def margin_product(messages, groups, gathered, tail):
    lanes = lane_ids()
    tail[...] = jnp.zeros(tail.shape, bf16)
    tail[0:64, 0:LANES] = gathered[256:320, :]
    tail[64:128, LANES : 2 * LANES] = gathered[256:320, :]
    total = jnp.zeros((BLOCK, LANES), f32)
    ends = jnp.zeros((BLOCK, LANES), f32)
    for message, group in zip(messages, groups):
        rows = jnp.concatenate([message[:, 0:BLOCK, :], message[:, BLOCK : 2 * BLOCK, :]], axis=-1)
        product = jnp.dot(rows.reshape(LIST * BLOCK, 256), gathered[0:256, :], preferred_element_type=f32)
        rest = message[:, 2 * BLOCK : MESSAGE, :].reshape(LIST * 48, LANES)
        second = jnp.dot(rest, tail[...], preferred_element_type=f32)
        for face in range(LIST):
            chosen = lanes == F_DEV + group * LIST + face
            total = jnp.where(chosen, product[face * BLOCK : (face + 1) * BLOCK], total)
            part = second[face * 48 : face * 48 + 40]
            ends = jnp.where(chosen, jnp.concatenate([part[:, 0:LANES], part[:, LANES:]], axis=0), ends)
    return total + ends


def pack_kernel(lists, rows, basis, out0, out1, out2, out3, latest, wide, ends, sem_latest, sems, sem_ends):
    first = pltpu.make_async_copy(basis.at[KRYLOV - 1], latest, sem_latest)
    first.start()
    outs = (out0, out1, out2, out3)
    numbers = sent_lists()
    copies = []
    for index in (2, 3, 1, 0):
        out, number = outs[index], numbers[index]
        for face in range(LIST):
            at = lists[number, face]
            slot = index * LIST + face
            copies.append(pltpu.make_async_copy(rows.at[at, :, pl.ds(256, LANES)], ends.at[slot], sem_ends.at[slot]))
            copies.append(
                pltpu.make_async_copy(rows.at[at, :, pl.ds(0, LANES)], out.at[face, pl.ds(0, BLOCK), :], sems.at[2 * slot])
            )
            copies.append(
                pltpu.make_async_copy(
                    rows.at[at, :, pl.ds(LANES, LANES)], out.at[face, pl.ds(BLOCK, BLOCK), :], sems.at[2 * slot + 1]
                )
            )
            for copy in copies[-3:]:
                copy.start()
    first.wait()
    wide[:, 0:BLOCK] = latest[...].astype(f32)
    wide[:, BLOCK:LANES] = jnp.zeros((F_DEV, LANES - BLOCK), f32)
    lanes = lax.broadcasted_iota(jnp.int32, (40, LANES), 1)
    for copy in copies:
        copy.wait()
    for index, out in enumerate(outs):
        for face in range(LIST):
            end = ends[index * LIST + face].astype(f32)
            both = jnp.where(lanes < 64, end[0:40], pltpu.roll(end[40:80], 64, 1))
            value = jnp.broadcast_to(wide[pl.ds(lists[numbers[index], face], 1), :], (8, LANES))
            out[face, 2 * BLOCK : MESSAGE, :] = jnp.concatenate([both, value], axis=0).astype(bf16)


def sweeps_kernel(
    rows, columns, margin_columns, lists, basis, m0, m1, m2, m3,
    precond_out, out0, out1, out2, out3, wide, ids, gathered, tail,
):
    fill_columns(columns, margin_columns, ids)
    factors = sweep_constants()
    messages, groups = (m0, m1, m2, m3), received_groups()
    wide[...] = jnp.zeros((LANES, LANES), f32)
    wide[0:F_DEV, 0:BLOCK] = basis[KRYLOV - 1].astype(f32)
    for message, group in zip(messages, groups):
        start = pl.multiple_of(F_DEV + group * LIST, LIST)
        last = [message[face, MESSAGE - 16 : MESSAGE, :].astype(f32)[8:9] for face in range(LIST)]
        wide[pl.ds(start, LIST), :] = jnp.concatenate(last, axis=0)
    residual = wide[...].T[0:BLOCK]
    direction = residual / center_value
    solution = direction
    for sweep in range(SWEEPS - 1):
        fill_gathered(direction.astype(bf16), ids, gathered)
        applied = own_product(rows, gathered)
        if sweep < SWEEPS - 2:
            applied = applied + margin_product(messages, groups, gathered, tail)
        residual = residual - applied
        keep_factor, push_factor = factors[sweep]
        direction = keep_factor * direction + push_factor * residual
        solution = solution + direction
    own = jnp.where(lane_ids() < F_DEV, solution, 0.0).astype(bf16)
    precond_out[...] = own
    wide[0:BLOCK, :] = own.astype(f32)
    wide[BLOCK:LANES, :] = jnp.zeros((LANES - BLOCK, LANES), f32)
    wide[...] = wide[...].T
    for out, number in zip((out0, out1, out2, out3), sent_lists()):
        for face in range(LIST):
            out[face : face + 1, :] = wide[pl.ds(lists[number, face], 1), :]


PAIRS = [(a, b) for a in range(KRYLOV) for b in range(a, KRYLOV)]
SUMS = KRYLOV + 1 + len(PAIRS)


def image_kernel(rows, columns, precond, g0, g1, g2, g3, basis, image_out, sums_out, wide, ids, gathered, sums):
    fill_columns(columns, None, ids)
    wide[...] = jnp.zeros((LANES, LANES), f32)
    for ghost, group in zip((g0, g1, g2, g3), received_groups()):
        wide[pl.ds(pl.multiple_of(F_DEV + group * LIST, LIST), LIST), :] = ghost[...]
    vector = precond[...] + wide[...].T[0:BLOCK].astype(bf16)
    fill_gathered(vector, ids, gathered)
    sums[...] = jnp.zeros((LANES, LANES), f32)
    spread = [basis[j].astype(f32) for j in range(KRYLOV)]
    for index, (a, b) in enumerate(PAIRS):
        row = KRYLOV + 1 + index
        sums[row : row + 1, 0:BLOCK] = jnp.sum(spread[a] * spread[b], axis=0, keepdims=True)
    product = own_product(rows, gathered)
    wide[0:BLOCK, :] = product
    wide[BLOCK:LANES, :] = jnp.zeros((LANES - BLOCK, LANES), f32)
    image = wide[...].T[0:F_DEV, 0:BLOCK]
    image_out[...] = image
    for j in range(KRYLOV):
        sums[j : j + 1, 0:BLOCK] = jnp.sum(spread[j] * image, axis=0, keepdims=True)
    sums[KRYLOV : KRYLOV + 1, 0:BLOCK] = jnp.sum(image * image, axis=0, keepdims=True)
    totals = jnp.sum(sums[...], axis=1, keepdims=True)
    row = jnp.broadcast_to(totals, (LANES, LANES)).T[0:1]
    sums_out[...] = jnp.broadcast_to(row, sums_out.shape)


def last_kernel(inverse_count, image, basis, sums, vector_out, projections_out):
    totals = jnp.sum(sums[...], axis=0, keepdims=True) * inverse_count
    entry = lambda index: totals[:, index : index + 1]
    heights = [entry(j) for j in range(KRYLOV)]
    squares = entry(KRYLOV)
    for index, (a, b) in enumerate(PAIRS):
        term = heights[a] * heights[b] * entry(KRYLOV + 1 + index)
        squares = squares + (term if a == b else 2.0 * term)
    for j in range(KRYLOV):
        squares = squares - 2.0 * heights[j] * heights[j]
    length = jnp.sqrt(squares + epsilon)
    remainder = image[...]
    for j in range(KRYLOV):
        remainder = remainder - heights[j] * basis[j].astype(f32)
    vector_out[...] = (remainder / length).astype(bf16)
    lanes = lax.broadcasted_iota(jnp.int32, (1, LANES), 1)
    row = jnp.where(lanes == KRYLOV, length, totals)
    projections_out[...] = row[0, 0 : KRYLOV + 1]


def shape(dims, dtype):
    return jax.ShapeDtypeStruct(dims, dtype)


def per_device(blocks, columns, margin_columns, send_lists, basis):
    devices = lax.axis_size("pitch") * lax.axis_size("span")
    columns_t = columns.T
    margin_t = margin_columns.T
    square = pltpu.VMEM((LANES, LANES), f32)
    ids = pltpu.VMEM((16, LANES), jnp.int32)
    gathered = pltpu.VMEM((WIDTH, LANES), bf16)

    messages = pl.pallas_call(
        pack_kernel,
        out_shape=[shape((LIST, MESSAGE, LANES), bf16)] * 4,
        in_specs=[SMEM, ANY, ANY],
        out_specs=[VMEM] * 4,
        scratch_shapes=[
            pltpu.VMEM((F_DEV, BLOCK), bf16),
            pltpu.VMEM((F_DEV, LANES), f32),
            pltpu.VMEM((4 * LIST, BLOCK, LANES), bf16),
            pltpu.SemaphoreType.DMA,
            pltpu.SemaphoreType.DMA((8 * LIST,)),
            pltpu.SemaphoreType.DMA((4 * LIST,)),
        ],
        compiler_params=PARAMS,
        name="pack",
    )(send_lists, blocks, basis)
    messages = exchange(messages)
    precond, *values = pl.pallas_call(
        sweeps_kernel,
        out_shape=[shape((BLOCK, LANES), bf16)] + [shape((LIST, LANES), f32)] * 4,
        in_specs=[VMEM, VMEM, VMEM, SMEM] + [VMEM] * 5,
        out_specs=[VMEM] * 5,
        scratch_shapes=[square, ids, gathered, pltpu.VMEM((LANES, 2 * LANES), bf16)],
        compiler_params=PARAMS,
        name="sweeps",
    )(blocks, columns_t, margin_t, send_lists, basis, *messages)
    ghosts = exchange(values)
    image, sums = pl.pallas_call(
        image_kernel,
        out_shape=[shape((F_DEV, BLOCK), f32), shape((devices, LANES), f32)],
        in_specs=[VMEM] * 8,
        out_specs=[VMEM] * 2,
        scratch_shapes=[square, ids, gathered, square],
        compiler_params=PARAMS,
        name="image",
    )(blocks, columns_t, precond, *ghosts, basis)
    sums = lax.all_to_all(sums.reshape(devices, 1, LANES), ("pitch", "span"), 0, 0)
    new_vector, projections = pl.pallas_call(
        functools.partial(last_kernel, 1.0 / (devices * F_DEV * BLOCK)),
        out_shape=[shape((F_DEV, BLOCK), bf16), shape((KRYLOV + 1,), f32)],
        in_specs=[VMEM] * 3,
        out_specs=[VMEM] * 2,
        name="new_vector",
    )(image, basis, sums.reshape(devices, LANES))
    return (new_vector, projections)


def solution(mesh):
    return jax.shard_map(
        per_device,
        mesh=mesh,
        in_specs=(
            P(("pitch", "span"), None, None),
            P(("pitch", "span"), None),
            P(("pitch", "span"), None),
            P(("pitch", "span"), None),
            P(None, ("pitch", "span"), None),
        ),
        out_specs=(P(("pitch", "span"), None), P()),
        check_vma=False,
    )
```

time: 168 us -> 78.8 us (0.47)
  Pallas kernels: 91.9 us -> 18.2 us
  starting transfers between devices: 26.1 us -> 15.9 us
  waiting for transfers between devices: 11.7 us -> 5.98 us
  local copies, waits for them, and re-layouts: 2.53 us -> 5.22 us
  blocking collectives: 34.7 us -> 32.5 us
    pallas_call x3 -> x1, Pallas kernels: 70 us -> 2.34 us  [per_device(): pl.pallas_call(pack_kernel, out_shape=[shape((LIST, MESSAGE, LANES), bf16...]
    ppermute x12 -> x8, starting transfers between devices: 26.1 us -> 15.9 us  [exchange(): received.append(lax.ppermute(value, axis, pairs))]
    ppermute x12 -> x8, waiting for transfers between devices: 11.7 us -> 5.98 us  [exchange(): received.append(lax.ppermute(value, axis, pairs))]
    unnamed x12 -> x20, local copies, waits for them, and re-layouts: 0.74 us -> 5.22 us
    pallas_call x1, Pallas kernels: 7.32 us -> 3.16 us  [per_device(): pl.pallas_call(image_kernel, out_shape=[shape((F_DEV, BLOCK), f32), shape...]
    all_to_all x1, blocking collectives: 34.7 us -> 32.5 us  [per_device(): lax.all_to_all(sums.reshape(devices, 1, LANES), ('pitch', 'span'), 0, 0)]
    squeeze x2 -> x0, local copies, waits for them, and re-layouts: 1.79 us -> none  [the longest x1 1.18 us: per_device(): return (new_vector, projections[0, 0:KRYLOV + 1])]
    pallas_call x1, Pallas kernels: 12.6 us -> 10.8 us  [per_device(): pl.pallas_call(sweeps_kernel, out_shape=[shape((BLOCK, LANES), bf16)] + [...]
  transfers between devices with their start and end apart: 12 -> 8, of which waited for: 5 -> 2; matrix products, arithmetic and copies ran while one was open for 0% -> 0% of each run, Pallas kernels for 5% -> 0%
where the time goes in v2:
time: 78.8 us; the launch traced here: 78.6 us
  blocking collectives  32.5 us (41%)
  Pallas kernels  18.2 us (23%)
  starting transfers between devices  15.9 us (20%)
  waiting for transfers between devices  5.98 us (8%)
  local copies, waits for them, and re-layouts  5.22 us (7%)
  between operations  0.79 us (1%)
    all_to_all x1, blocking collectives, per_device(): lax.all_to_all(sums.reshape(devices, 1, LANES), ('pitch', 'span'), 0, 0)  32.5 us
    ppermute x8, starting transfers between devices, exchange(): received.append(lax.ppermute(value, axis, pairs))  15.9 us
    pallas_call x1, Pallas kernels, per_device(): pl.pallas_call(sweeps_kernel, out_shape=[shape((BLOCK, LANES), bf16)] + [...  10.8 us
    ppermute x8, waiting for transfers between devices, exchange(): received.append(lax.ppermute(value, axis, pairs))  5.98 us
    unnamed x20, local copies, waits for them, and re-layouts  5.22 us
    pallas_call x1, Pallas kernels, per_device(): pl.pallas_call(image_kernel, out_shape=[shape((F_DEV, BLOCK), f32), shape...  3.16 us
    pallas_call x1, Pallas kernels, per_device(): pl.pallas_call(pack_kernel, out_shape=[shape((LIST, MESSAGE, LANES), bf16...  2.34 us
    pallas_call x1, Pallas kernels, per_device(): pl.pallas_call(functools.partial(last_kernel, 1.0 / (devices * F_DEV * BL...  1.95 us
  transfers between devices with their start and end apart: 8, of which 2 were waited for; matrix products, arithmetic and copies ran while one was open for 0% of the time, Pallas kernels for 0%

profile of v2, /device:TPU:1, one launch (start us, length us, event | category | flops | bytes accessed | tf_op | source)
XLA Modules:
  0.0 78.6 jit_solution(1659587348456351667)
XLA Ops:
  0.6 0.0 copy-start
  0.6 3.6 %copy-done = bf16[64,80,880]{2,1,0:T(8,128)(2,1)S(1)} copy-done((bf16[64,80,880]{2,1,0:T(8,128)(2,1)S(1)}, bf16[64,80,880]{2,1,0:T(8,128)(2,1)}, u32[]{:S(2)}) %copy-start) | copy-done | bytes 9011224
  4.2 0.0 copy-start.1
  4.2 0.9 %copy-done.1 = bf16[8,64,80]{2,1,0:T(8,128)(2,1)S(1)} copy-done((bf16[8,64,80]{2,1,0:T(8,128)(2,1)S(1)}, bf16[8,64,80]{2,1,0:T(8,128)(2,1)}, u32[]{:S(2)}) %copy-start.1) | copy-done | bytes 81944
  5.1 0.0 copy-start.5
  5.1 0.7 copy-done.5
  5.8 0.0 copy-start.4
  5.8 0.0 copy-start.6
  5.8 0.0 slice-start
  5.8 0.0 slice-start.1
  5.8 0.0 copy-start.2
  5.8 2.3 %pack.1 = (bf16[8,208,128]{2,1,0:T(8,128)(2,1)S(1)}, bf16[8,208,128]{2,1,0:T(8,128)(2,1)S(1)}, bf16[8,208,128]{2,1,0:T(8,128)(2,1)S(1)}, bf16[8,208,128]{2,1,0:T(8,128)(2,1)S(1)}) custom-call(s32[4,8]{1,0:T(4,128)S(1)} %copy-done.5, bf16[64,80,880]{2,1,0:T(8,128)(2,1)S(1)} %copy-done, bf16[8,64,80]{2,1,0:T(8,128)(2,1)S(1)} %copy-done.1), custom_call_target="tpu_custom_call" | custom-call | tf_op jit(solution)/shard_map/pack/pallas_call | solution.py:258
  8.2 3.3 %collective-permute-start = (bf16[8,208,128]{2,1,0:T(8,128)(2,1)S(1)}, bf16[8,208,128]{2,1,0:T(8,128)(2,1)S(1)}, u32[]{:S(2)}, u32[]{:S(2)}) collective-permute-start(bf16[8,208,128]{2,1,0:T(8,128)(2,1)S(1)} %get-tuple-element.13), channel_id=1, source_target_pairs={{0,16},{16,0},{32,48},{48,32},{64,80},{80,64},{96,112},{112,96},{1... | collective-permute-start | bytes 1277960 | tf_op jit(solution)/shard_map/ppermute | solution.py:70
  11.5 0.0 collective-permute-start.1
  11.5 1.1 %collective-permute-start.2 = (bf16[8,208,128]{2,1,0:T(8,128)(2,1)S(1)}, bf16[8,208,128]{2,1,0:T(8,128)(2,1)S(1)}, u32[]{:S(2)}, u32[]{:S(2)}) collective-permute-start(bf16[8,208,128]{2,1,0:T(8,128)(2,1)S(1)} %get-tuple-element.15), channel_id=1, source_target_pairs={{0,1},{1,0},{2,3},{3,2},{4,5},{5,4},{6,7},{7,6},{8,9},{9,8},{10,11... | collective-permute-start | bytes 1277960 | tf_op jit(solution)/shard_map/ppermute | solution.py:70
  12.6 0.9 %collective-permute-start.3 = (bf16[8,208,128]{2,1,0:T(8,128)(2,1)S(1)}, bf16[8,208,128]{2,1,0:T(8,128)(2,1)S(1)}, u32[]{:S(2)}, u32[]{:S(2)}) collective-permute-start(bf16[8,208,128]{2,1,0:T(8,128)(2,1)S(1)} %get-tuple-element.16), channel_id=1, source_target_pairs={{1,2},{2,1},{3,4},{4,3},{5,6},{6,5},{7,8},{8,7},{9,10},{10,9},{11,... | collective-permute-start | bytes 1277960 | tf_op jit(solution)/shard_map/ppermute | solution.py:70
  13.5 0.0 collective-permute-done.m0
  13.5 5.9 %collective-permute-done.1.m1 = bf16[8,208,128]{2,1,0:T(8,128)(2,1)S(1)} collective-permute-done((bf16[8,208,128]{2,1,0:T(8,128)(2,1)S(1)}, bf16[8,208,128]{2,1,0:T(8,128)(2,1)S(1)}, u32[]{:S(2)}, u32[]{:S(2)}) %collective-permute-start.1) | collective-permute-done | bytes 426016 | tf_op jit(solution)/shard_map/ppermute | solution.py:70
  19.4 0.0 collective-permute-done.2.m2
  19.4 0.0 collective-permute-done.3.m3
  19.4 0.0 copy-done.4
  19.4 0.0 copy-done.6
  19.4 0.0 slice-start.2
  19.4 10.8 %sweeps.1 = (bf16[80,128]{1,0:T(8,128)(2,1)S(1)}, f32[8,128]{1,0:T(8,128)S(1)}, f32[8,128]{1,0:T(8,128)S(1)}, f32[8,128]{1,0:T(8,128)S(1)}, f32[8,128]{1,0:T(8,128)S(1)}) custom-call(bf16[64,80,880]{2,1,0:T(8,128)(2,1)S(1)} %copy-done, s32[11,64]{1,0:T(8,128)S(1)} %bitcast.9, s32[4,32]{1,0:T(4,128)S(1)} %bitcast.11, s32[4,8]{1,0:T(4,128)S(1)} %copy-done.5, ...), custom_call_target="tpu_custom_call" | custom-call | tf_op jit(solution)/shard_map/sweeps/pallas_call | solution.py:275
  30.2 4.6 %collective-permute-start.4 = (f32[8,128]{1,0:T(8,128)S(1)}, f32[8,128]{1,0:T(8,128)S(1)}, u32[]{:S(2)}, u32[]{:S(2)}) collective-permute-start(f32[8,128]{1,0:T(8,128)S(1)} %get-tuple-element.18), channel_id=1, source_target_pairs={{0,16},{16,0},{32,48},{48,32},{64,80},{80,64},{96,112},{112,96},{1... | collective-permute-start | bytes 12296 | tf_op jit(solution)/shard_map/ppermute | solution.py:70
  34.8 1.4 %collective-permute-start.5 = (f32[8,128]{1,0:T(8,128)S(1)}, f32[8,128]{1,0:T(8,128)S(1)}, u32[]{:S(2)}, u32[]{:S(2)}) collective-permute-start(f32[8,128]{1,0:T(8,128)S(1)} %get-tuple-element.19), channel_id=1, source_target_pairs={{16,32},{32,16},{48,64},{64,48},{80,96},{96,80},{112,128},{128,112... | collective-permute-start | bytes 12296 | tf_op jit(solution)/shard_map/ppermute | solution.py:70
  36.2 3.7 %collective-permute-start.6 = (f32[8,128]{1,0:T(8,128)S(1)}, f32[8,128]{1,0:T(8,128)S(1)}, u32[]{:S(2)}, u32[]{:S(2)}) collective-permute-start(f32[8,128]{1,0:T(8,128)S(1)} %get-tuple-element.20), channel_id=1, source_target_pairs={{0,1},{1,0},{2,3},{3,2},{4,5},{5,4},{6,7},{7,6},{8,9},{9,8},{10,11... | collective-permute-start | bytes 12296 | tf_op jit(solution)/shard_map/ppermute | solution.py:70
  39.9 0.9 %collective-permute-start.7 = (f32[8,128]{1,0:T(8,128)S(1)}, f32[8,128]{1,0:T(8,128)S(1)}, u32[]{:S(2)}, u32[]{:S(2)}) collective-permute-start(f32[8,128]{1,0:T(8,128)S(1)} %get-tuple-element.21), channel_id=1, source_target_pairs={{1,2},{2,1},{3,4},{4,3},{5,6},{6,5},{7,8},{8,7},{9,10},{10,9},{11,... | collective-permute-start | bytes 12296 | tf_op jit(solution)/shard_map/ppermute | solution.py:70
  40.8 0.0 collective-permute-done.4.g0
  40.8 0.0 collective-permute-done.5.g1
  40.8 0.1 collective-permute-done.6.g2
  40.9 0.0 collective-permute-done.7.g3
  40.9 0.0 slice-done
  40.9 0.0 slice-done.1
  40.9 0.0 copy-done.2
  40.9 0.0 slice-done.2
  41.0 3.2 %image.1 = (f32[64,80]{1,0:T(8,128)S(1)}, f32[256,128]{1,0:T(8,128)S(1)}) custom-call(bf16[64,80,880]{2,1,0:T(8,128)(2,1)S(1)} %bitcast.7, s32[11,64]{1,0:T(8,128)S(1)} %bitcast.10, bf16[80,128]{1,0:T(8,128)(2,1)S(1)} %get-tuple-element.17.precond, f32[8,128]{1,0:T(8,128)S(1)} %collective-permute-done.4.g0, f32[8,128]{1,0:T(8,128)S(1)} %collective-permute-done.5.g1, ...), custom_call_target="tpu_custom_call" | custom-call | tf_op jit(solution)/shard_map/image/pallas_call | solution.py:285
  44.2 0.0 copy-start.3
  44.2 32.5 %all_to_all.5 = f32[256,1,128]{2,1,0:T(1,128)} all-to-all(f32[256,1,128]{2,1,0:T(1,128)S(1)} %bitcast.8), channel_id=1, replica_groups=mesh['pitch'=16,'span'=16] {'pitch','span'}, dimensions={0} | all-to-all | bytes 262144 | tf_op jit(solution)/shard_map/all_to_all | solution.py:294
  76.6 0.0 copy-done.3
  76.6 1.9 %new_vector.1 = (bf16[64,80]{1,0:T(8,128)(2,1)}, f32[9]{0:T(128)}) custom-call(f32[64,80]{1,0:T(8,128)} %copy-done.3, bf16[8,64,80]{2,1,0:T(8,128)(2,1)} %basis.7, f32[256,128]{1,0:T(8,128)} %bitcast.12), custom_call_target="tpu_custom_call" | custom-call | tf_op jit(solution)/shard_map/new_vector/pallas_call | solution.py:295
  (1 shorter events, 0.0 us)
Async XLA Ops:
  0.6 3.6 %copy-start = (bf16[64,80,880]{2,1,0:T(8,128)(2,1)S(1)}, bf16[64,80,880]{2,1,0:T(8,128)(2,1)}, u32[]{:S(2)}) copy-start(bf16[64,80,880]{2,1,0:T(8,128)(2,1)} %rows.5) | copy-start | bytes 27033604
  4.2 0.9 %copy-start.1 = (bf16[8,64,80]{2,1,0:T(8,128)(2,1)S(1)}, bf16[8,64,80]{2,1,0:T(8,128)(2,1)}, u32[]{:S(2)}) copy-start(bf16[8,64,80]{2,1,0:T(8,128)(2,1)} %basis.7) | copy-start | bytes 245764
  5.1 0.7 copy-start.5
  5.8 13.6 %copy-start.4 = (s32[64,11]{0,1:T(8,128)S(1)}, s32[64,11]{0,1:T(8,128)}, u32[]{:S(2)}) copy-start(s32[64,11]{0,1:T(8,128)} %param.6) | copy-start | bytes 8452
  5.8 13.6 %copy-start.6 = (s32[32,4]{0,1:T(4,128)S(1)}, s32[32,4]{0,1:T(4,128)}, u32[]{:S(2)}) copy-start(s32[32,4]{0,1:T(4,128)} %param.7) | copy-start | bytes 1540
  5.8 35.1 %slice-start = ((s8[9175040]{0:T(1024)(128)(4,1)}), s8[4194304]{0:T(1024)(128)(4,1)S(1)}, s32[]{:S(2)}) async-start(s8[9175040]{0:T(1024)(128)(4,1)} %bitcast.6), calls=%async_computation.1 | async-start | bytes 8388608
  5.8 35.1 %slice-start.1 = ((s8[9175040]{0:T(1024)(128)(4,1)}), s8[4194304]{0:T(1024)(128)(4,1)S(1)}, s32[]{:S(2)}) async-start(s8[9175040]{0:T(1024)(128)(4,1)} %bitcast.6), calls=%async_computation.2 | async-start | bytes 8388608
  5.8 35.1 %copy-start.2 = (bf16[8,64,80]{2,1,0:T(8,128)(2,1)S(1)}, bf16[8,64,80]{2,1,0:T(8,128)(2,1)}, u32[]{:S(2)}) copy-start(bf16[8,64,80]{2,1,0:T(8,128)(2,1)} %basis.7) | copy-start | bytes 245764
  8.2 5.3 %collective-permute-start = (bf16[8,208,128]{2,1,0:T(8,128)(2,1)S(1)}, bf16[8,208,128]{2,1,0:T(8,128)(2,1)S(1)}, u32[]{:S(2)}, u32[]{:S(2)}) collective-permute-start(bf16[8,208,128]{2,1,0:T(8,128)(2,1)S(1)} %get-tuple-element.13), channel_id=1, source_target_pairs={{0,16},{16,0},{32,48},{48,32},{64,80},{80,64},{96,112},{112,96},{1... | collective-permute-start | bytes 1277960 | tf_op jit(solution)/shard_map/ppermute | solution.py:70
  11.5 7.8 %collective-permute-start.1 = (bf16[8,208,128]{2,1,0:T(8,128)(2,1)S(1)}, bf16[8,208,128]{2,1,0:T(8,128)(2,1)S(1)}, u32[]{:S(2)}, u32[]{:S(2)}) collective-permute-start(bf16[8,208,128]{2,1,0:T(8,128)(2,1)S(1)} %get-tuple-element.14), channel_id=1, source_target_pairs={{16,32},{32,16},{48,64},{64,48},{80,96},{96,80},{112,128},{128,112... | collective-permute-start | bytes 1277960 | tf_op jit(solution)/shard_map/ppermute | solution.py:70
  11.5 7.8 %collective-permute-start.2 = (bf16[8,208,128]{2,1,0:T(8,128)(2,1)S(1)}, bf16[8,208,128]{2,1,0:T(8,128)(2,1)S(1)}, u32[]{:S(2)}, u32[]{:S(2)}) collective-permute-start(bf16[8,208,128]{2,1,0:T(8,128)(2,1)S(1)} %get-tuple-element.15), channel_id=1, source_target_pairs={{0,1},{1,0},{2,3},{3,2},{4,5},{5,4},{6,7},{7,6},{8,9},{9,8},{10,11... | collective-permute-start | bytes 1277960 | tf_op jit(solution)/shard_map/ppermute | solution.py:70
  12.6 6.8 %collective-permute-start.3 = (bf16[8,208,128]{2,1,0:T(8,128)(2,1)S(1)}, bf16[8,208,128]{2,1,0:T(8,128)(2,1)S(1)}, u32[]{:S(2)}, u32[]{:S(2)}) collective-permute-start(bf16[8,208,128]{2,1,0:T(8,128)(2,1)S(1)} %get-tuple-element.16), channel_id=1, source_target_pairs={{1,2},{2,1},{3,4},{4,3},{5,6},{6,5},{7,8},{8,7},{9,10},{10,9},{11,... | collective-permute-start | bytes 1277960 | tf_op jit(solution)/shard_map/ppermute | solution.py:70
  19.4 21.6 %slice-start.2 = ((s8[9175040]{0:T(1024)(128)(4,1)}), s8[786432]{0:T(1024)(128)(4,1)S(1)}, s32[]{:S(2)}) async-start(s8[9175040]{0:T(1024)(128)(4,1)} %bitcast.6), calls=%async_computation.3 | async-start | bytes 1572864
  30.2 10.6 %collective-permute-start.4 = (f32[8,128]{1,0:T(8,128)S(1)}, f32[8,128]{1,0:T(8,128)S(1)}, u32[]{:S(2)}, u32[]{:S(2)}) collective-permute-start(f32[8,128]{1,0:T(8,128)S(1)} %get-tuple-element.18), channel_id=1, source_target_pairs={{0,16},{16,0},{32,48},{48,32},{64,80},{80,64},{96,112},{112,96},{1... | collective-permute-start | bytes 12296 | tf_op jit(solution)/shard_map/ppermute | solution.py:70
  34.8 6.0 %collective-permute-start.5 = (f32[8,128]{1,0:T(8,128)S(1)}, f32[8,128]{1,0:T(8,128)S(1)}, u32[]{:S(2)}, u32[]{:S(2)}) collective-permute-start(f32[8,128]{1,0:T(8,128)S(1)} %get-tuple-element.19), channel_id=1, source_target_pairs={{16,32},{32,16},{48,64},{64,48},{80,96},{96,80},{112,128},{128,112... | collective-permute-start | bytes 12296 | tf_op jit(solution)/shard_map/ppermute | solution.py:70
  36.2 4.7 %collective-permute-start.6 = (f32[8,128]{1,0:T(8,128)S(1)}, f32[8,128]{1,0:T(8,128)S(1)}, u32[]{:S(2)}, u32[]{:S(2)}) collective-permute-start(f32[8,128]{1,0:T(8,128)S(1)} %get-tuple-element.20), channel_id=1, source_target_pairs={{0,1},{1,0},{2,3},{3,2},{4,5},{5,4},{6,7},{7,6},{8,9},{9,8},{10,11... | collective-permute-start | bytes 12296 | tf_op jit(solution)/shard_map/ppermute | solution.py:70
  39.9 1.0 %collective-permute-start.7 = (f32[8,128]{1,0:T(8,128)S(1)}, f32[8,128]{1,0:T(8,128)S(1)}, u32[]{:S(2)}, u32[]{:S(2)}) collective-permute-start(f32[8,128]{1,0:T(8,128)S(1)} %get-tuple-element.21), channel_id=1, source_target_pairs={{1,2},{2,1},{3,4},{4,3},{5,6},{6,5},{7,8},{8,7},{9,10},{10,9},{11,... | collective-permute-start | bytes 12296 | tf_op jit(solution)/shard_map/ppermute | solution.py:70
  44.2 32.5 %copy-start.3 = (f32[64,80]{1,0:T(8,128)}, f32[64,80]{1,0:T(8,128)S(1)}, u32[]{:S(2)}) copy-start(f32[64,80]{1,0:T(8,128)S(1)} %get-tuple-element.22.image) | copy-start | bytes 61444

commit v3 on v2

v3 whole, which is shorter than its diff:
```python
import functools

import jax
import jax.numpy as jnp
from jax import lax
from jax.experimental import pallas as pl
from jax.experimental.pallas import tpu as pltpu
from jax.sharding import PartitionSpec as P

BLOCK = 80
SLOTS = 11
GSLOTS = 4
F_DEV = 64
KRYLOV = 8
SWEEPS = 4
LIST = 8
LANES = 128
WIDTH = SLOTS * BLOCK
LEAD = 384
MESSAGE = 208
GRAM = 64
GUARD = 2.0**-11
KTILES = ((0, 256), (256, 512), (512, 768), (768, 880))
REST = 768
SPLIT = 24

center_value = 1.0
half_width = 0.5
epsilon = 1e-06

f32 = jnp.float32
bf16 = jnp.bfloat16
VMEM = pl.BlockSpec(memory_space=pltpu.VMEM)
SMEM = pl.BlockSpec(memory_space=pltpu.SMEM)
ANY = pl.BlockSpec(memory_space=pl.ANY)
PARAMS = pltpu.CompilerParams(vmem_limit_bytes=32 * 2**20)
PACK_PARAMS = pltpu.CompilerParams(vmem_limit_bytes=58 * 2**20)


def sweep_constants():
    stretch = center_value / half_width
    ratio_now = 1.0 / stretch
    factors = []
    for _ in range(SWEEPS - 1):
        ratio_next = 1.0 / (2.0 * stretch - ratio_now)
        factors.append((ratio_next * ratio_now, 2.0 * ratio_next / half_width))
        ratio_now = ratio_next
    return factors


def positions():
    return lax.axis_index("pitch") % 2, lax.axis_index("span") % 2


def sent_lists():
    pitch_odd, span_odd = positions()
    return pitch_odd, 1 - pitch_odd, 2 + span_odd, 3 - span_odd


def received_groups():
    pitch_odd, span_odd = positions()
    span = lax.axis_index("span")
    inside = (span != 0) & (span != lax.axis_size("span") - 1)
    return (1 - pitch_odd, True), (pitch_odd, True), (3 - span_odd, True), (2 + span_odd, inside)


def exchange(outgoing):
    received = [None] * 4
    for index in (3, 2, 1, 0):
        axis = "pitch" if index < 2 else "span"
        devices = lax.axis_size(axis)
        pairs = []
        for low in range(index % 2, devices, 2):
            high = (low + 1) % devices
            pairs += [(low, high), (high, low)]
        received[index] = lax.ppermute(outgoing[index], axis, pairs)
    return received


def lane_ids():
    return lax.broadcasted_iota(jnp.int32, (BLOCK, LANES), 1)


def choose_kernel(rows, columns, margin_columns, chosen, ids):
    ids[...] = jnp.full(ids.shape, LANES - 1, jnp.int32)
    ids[0:SLOTS, 0:F_DEV] = columns[...]
    ids[0:GSLOTS, F_DEV : F_DEV + 4 * LIST] = margin_columns[...]
    positions = lax.broadcasted_iota(jnp.int32, (LANES, LANES), 0)
    for slot in range(SLOTS):
        here = positions == ids[slot : slot + 1, :]
        chosen[:, slot * LANES : (slot + 1) * LANES] = here.astype(f32).astype(bf16)


def fill_gathered(vector, chosen, gathered):
    product = jnp.dot(vector, chosen[...], preferred_element_type=f32).astype(bf16)
    for slot in range(SLOTS):
        gathered[slot * BLOCK : (slot + 1) * BLOCK, :] = product[:, slot * LANES : (slot + 1) * LANES]


def own_product(rows_ref, gathered, turned):
    lanes = lane_ids()
    for start in range(0, WIDTH, LANES):
        stop = min(start + LANES, WIDTH)
        turned[:, start:stop] = gathered[start:stop, :].astype(f32).T
    total = jnp.zeros((BLOCK, LANES), f32)
    for start, stop in KTILES:
        rows = rows_ref[0:SPLIT, :, start:stop].reshape(SPLIT * BLOCK, stop - start)
        product = jnp.dot(rows, gathered[start:stop, :], preferred_element_type=f32)
        part = jnp.zeros((BLOCK, LANES), f32)
        for face in range(SPLIT):
            part = jnp.where(lanes == face, product[face * BLOCK : (face + 1) * BLOCK], part)
        total = total + part
    for face in range(SPLIT, F_DEV):
        row = turned[face : face + 1, :]
        block_row = rows_ref[face].astype(f32)
        part = jnp.zeros((BLOCK, LANES), f32)
        for start in range(0, REST, LANES):
            part = part + block_row[:, start : start + LANES] * row[:, start : start + LANES]
        value = jnp.sum(part, axis=1, keepdims=True)
        value = value + jnp.sum(block_row[:, REST:WIDTH] * row[:, REST:WIDTH], axis=1, keepdims=True)
        total = jnp.where(lanes == face, value, total)
    return total


def margin_product(messages, groups, gathered, tail):
    lanes = lane_ids()
    tail[...] = jnp.zeros(tail.shape, bf16)
    tail[0:64, 0:LANES] = gathered[256:320, :]
    tail[64:128, LANES : 2 * LANES] = gathered[256:320, :]
    total = jnp.zeros((BLOCK, LANES), f32)
    ends = jnp.zeros((BLOCK, LANES), f32)
    for message, (group, there) in zip(messages, groups):
        rows = jnp.concatenate([message[:, 0:BLOCK, :], message[:, BLOCK : 2 * BLOCK, :]], axis=-1)
        product = jnp.dot(rows.reshape(LIST * BLOCK, 256), gathered[0:256, :], preferred_element_type=f32)
        rest = message[:, 2 * BLOCK : MESSAGE, :].reshape(LIST * 48, LANES)
        second = jnp.dot(rest, tail[...], preferred_element_type=f32)
        for face in range(LIST):
            chosen = (lanes == F_DEV + group * LIST + face) & there
            total = jnp.where(chosen, product[face * BLOCK : (face + 1) * BLOCK], total)
            part = second[face * 48 : face * 48 + 40]
            ends = jnp.where(chosen, jnp.concatenate([part[:, 0:LANES], part[:, LANES:]], axis=0), ends)
    return total + ends


def pack_kernel(indices, lists, rows, basis, out0, out1, latest, wide, staged, sem_latest, sems):
    first = pltpu.make_async_copy(basis.at[KRYLOV - 1], latest, sem_latest)
    first.start()
    outs = (out0, out1)
    numbers = [sent_lists()[index] for index in indices]
    copies = []
    for place in range(2):
        for face in range(LIST):
            slot = place * LIST + face
            source = rows.at[lists[numbers[place], face], :, pl.ds(0, LEAD)]
            copies.append(pltpu.make_async_copy(source, staged.at[slot], sems.at[slot]))
            copies[-1].start()
    first.wait()
    wide[:, 0:BLOCK] = latest[...].astype(f32)
    wide[:, BLOCK:LANES] = jnp.zeros((F_DEV, LANES - BLOCK), f32)
    lanes = lax.broadcasted_iota(jnp.int32, (40, LANES), 1)
    for place, out in enumerate(outs):
        for face in range(LIST):
            copies[place * LIST + face].wait()
        for face in range(LIST):
            slot = place * LIST + face
            out[face, 0:BLOCK, :] = staged[slot, :, 0:LANES]
            out[face, BLOCK : 2 * BLOCK, :] = staged[slot, :, LANES : 2 * LANES]
            end = staged[slot, :, 2 * LANES : LEAD].astype(f32)
            both = jnp.where(lanes < 64, end[0:40], pltpu.roll(end[40:80], 64, 1))
            value = jnp.broadcast_to(wide[pl.ds(lists[numbers[place], face], 1), :], (8, LANES))
            out[face, 2 * BLOCK : MESSAGE, :] = jnp.concatenate([both, value], axis=0).astype(bf16)


def pack(indices, send_lists, blocks, basis):
    return pl.pallas_call(
        functools.partial(pack_kernel, indices),
        out_shape=[shape((LIST, MESSAGE, LANES), bf16)] * 2,
        in_specs=[SMEM, ANY, ANY],
        out_specs=[VMEM] * 2,
        scratch_shapes=[
            pltpu.VMEM((F_DEV, BLOCK), bf16),
            pltpu.VMEM((F_DEV, LANES), f32),
            pltpu.VMEM((2 * LIST, BLOCK, LEAD), bf16),
            pltpu.SemaphoreType.DMA,
            pltpu.SemaphoreType.DMA((2 * LIST,)),
        ],
        compiler_params=PACK_PARAMS,
        name="pack_span" if indices[0] > 1 else "pack_pitch",
    )(send_lists, blocks, basis)


def sweeps_kernel(
    rows, chosen, lists, basis, m3, m2, m1, m0,
    precond_out, out0, out1, out2, out3, wide, gathered, turned, tail,
):
    factors = sweep_constants()
    messages, groups = (m0, m1, m2, m3), received_groups()
    wide[...] = jnp.zeros((LANES, LANES), f32)
    wide[0:F_DEV, 0:BLOCK] = basis[KRYLOV - 1].astype(f32)
    for message, (group, there) in zip(messages, groups):
        start = pl.multiple_of(F_DEV + group * LIST, LIST)
        last = [message[face, MESSAGE - 16 : MESSAGE, :].astype(f32)[8:9] for face in range(LIST)]
        wide[pl.ds(start, LIST), :] = jnp.where(there, jnp.concatenate(last, axis=0), 0.0)
    residual = wide[...].T[0:BLOCK]
    direction = residual / center_value
    solution = direction
    for sweep in range(SWEEPS - 1):
        fill_gathered(direction.astype(bf16), chosen, gathered)
        applied = own_product(rows, gathered, turned)
        if sweep < SWEEPS - 2:
            applied = applied + margin_product(messages, groups, gathered, tail)
        residual = residual - applied
        keep_factor, push_factor = factors[sweep]
        direction = keep_factor * direction + push_factor * residual
        solution = solution + direction
    own = jnp.where(lane_ids() < F_DEV, solution, 0.0).astype(bf16)
    precond_out[...] = own
    wide[0:BLOCK, :] = own.astype(f32)
    wide[BLOCK:LANES, :] = jnp.zeros((LANES - BLOCK, LANES), f32)
    wide[...] = wide[...].T
    for out, number in zip((out0, out1, out2, out3), sent_lists()):
        for face in range(LIST):
            out[face : face + 1, :] = wide[pl.ds(lists[number, face], 1), :]


def image_kernel(
    rows, chosen, precond, g3, g2, g1, g0, basis, image_out, sums_out, wide, gathered, turned, sums
):
    wide[...] = jnp.zeros((LANES, LANES), f32)
    for ghost, (group, there) in zip((g0, g1, g2, g3), received_groups()):
        wide[pl.ds(pl.multiple_of(F_DEV + group * LIST, LIST), LIST), :] = jnp.where(there, ghost[...], 0.0)
    vector = precond[...] + wide[...].T[0:BLOCK].astype(bf16)
    fill_gathered(vector, chosen, gathered)
    sums[...] = jnp.zeros((LANES, LANES), f32)
    spread = [basis[j].astype(f32) for j in range(KRYLOV)]
    for a in range(KRYLOV):
        for b in range(a, KRYLOV):
            entry = jnp.sum(spread[a] * spread[b], axis=0, keepdims=True)
            for row in {GRAM + KRYLOV * a + b, GRAM + KRYLOV * b + a}:
                sums[row : row + 1, 0:BLOCK] = entry
    product = own_product(rows, gathered, turned)
    wide[0:BLOCK, :] = product
    wide[BLOCK:LANES, :] = jnp.zeros((LANES - BLOCK, LANES), f32)
    image = wide[...].T[0:F_DEV, 0:BLOCK]
    image_out[...] = image
    for j in range(KRYLOV):
        sums[j : j + 1, 0:BLOCK] = jnp.sum(spread[j] * image, axis=0, keepdims=True)
    sums[KRYLOV : KRYLOV + 1, 0:BLOCK] = jnp.sum(image * image, axis=0, keepdims=True)
    totals = jnp.sum(sums[...], axis=1, keepdims=True)
    row = jnp.broadcast_to(totals, (LANES, LANES)).T[0:1]
    sums_out[...] = jnp.broadcast_to(row, sums_out.shape)


def last_kernel(inverse_count, image, basis, sums, vector_out, projections_out, remainder_out, flag_out):
    totals = jnp.sum(sums[...], axis=0, keepdims=True) * inverse_count
    lanes = lax.broadcasted_iota(jnp.int32, (KRYLOV, LANES), 1)
    rows = lax.broadcasted_iota(jnp.int32, (KRYLOV, LANES), 0)
    heights = jnp.broadcast_to(totals, (LANES, LANES)).T[0:KRYLOV]
    left = jnp.sum(jnp.where(lanes // KRYLOV - GRAM // KRYLOV == rows, heights, 0.0), axis=0, keepdims=True)
    right = jnp.sum(jnp.where(lanes % KRYLOV == rows, heights, 0.0), axis=0, keepdims=True)
    lane = lanes[0:1]
    terms = jnp.where(lane < KRYLOV, -2.0 * totals * totals, jnp.where(lane == KRYLOV, totals, left * right * totals))
    total = totals[:, KRYLOV : KRYLOV + 1]
    squares = jnp.sum(terms, axis=1, keepdims=True)
    length = jnp.sqrt(jnp.maximum(squares, 0.0) + epsilon)
    remainder = image[...]
    for j in range(KRYLOV):
        remainder = remainder - heights[j : j + 1, 0:BLOCK] * basis[j].astype(f32)
    remainder_out[...] = remainder
    vector_out[...] = (remainder / length).astype(bf16)
    projections_out[...] = jnp.where(lane == KRYLOV, length, totals)[0, 0 : KRYLOV + 1]
    flag_out[0] = jnp.where(squares < GUARD * total, 1, 0)[0, 0]


def shape(dims, dtype):
    return jax.ShapeDtypeStruct(dims, dtype)


def per_device(blocks, columns, margin_columns, send_lists, basis):
    devices = lax.axis_size("pitch") * lax.axis_size("span")
    square = pltpu.VMEM((LANES, LANES), f32)
    gathered = pltpu.VMEM((WIDTH, LANES), bf16)
    turned = pltpu.VMEM((LANES, WIDTH), f32)

    last, third = pack((3, 2), send_lists, blocks, basis)
    second, first = pack((1, 0), send_lists, blocks, basis)
    messages = exchange([first, second, third, last])
    chosen = pl.pallas_call(
        choose_kernel,
        out_shape=shape((LANES, SLOTS * LANES), bf16),
        in_specs=[VMEM] * 3,
        out_specs=VMEM,
        scratch_shapes=[pltpu.VMEM((16, LANES), jnp.int32)],
        compiler_params=PARAMS,
        cost_estimate=pl.CostEstimate(flops=0, bytes_accessed=2**20, transcendentals=0),
        name="choose",
    )(blocks, columns.T, margin_columns.T)
    precond, *values = pl.pallas_call(
        sweeps_kernel,
        out_shape=[shape((BLOCK, LANES), bf16)] + [shape((LIST, LANES), f32)] * 4,
        in_specs=[VMEM, VMEM, SMEM] + [VMEM] * 5,
        out_specs=[VMEM] * 5,
        scratch_shapes=[square, gathered, turned, pltpu.VMEM((LANES, 2 * LANES), bf16)],
        compiler_params=PARAMS,
        name="sweeps",
    )(blocks, chosen, send_lists, basis, *messages[::-1])
    ghosts = exchange(values)
    image, sums = pl.pallas_call(
        image_kernel,
        out_shape=[shape((F_DEV, BLOCK), f32), shape((devices, LANES), f32)],
        in_specs=[VMEM] * 8,
        out_specs=[VMEM] * 2,
        scratch_shapes=[square, gathered, turned, square],
        compiler_params=PARAMS,
        name="image",
    )(blocks, chosen, precond, *ghosts[::-1], basis)
    sums = lax.all_to_all(sums.reshape(devices, 1, LANES), ("pitch", "span"), 0, 0)
    inverse_count = 1.0 / (devices * F_DEV * BLOCK)
    new_vector, projections, remainder, cancelled = pl.pallas_call(
        functools.partial(last_kernel, inverse_count),
        out_shape=[
            shape((F_DEV, BLOCK), bf16),
            shape((KRYLOV + 1,), f32),
            shape((F_DEV, BLOCK), f32),
            shape((1,), jnp.int32),
        ],
        in_specs=[VMEM] * 3,
        out_specs=[VMEM] * 3 + [SMEM],
        name="new_vector",
    )(image, basis, sums.reshape(devices, LANES))

    def summed_again(state):
        squares = lax.psum(jnp.sum(remainder * remainder), ("pitch", "span")) * inverse_count
        length = jnp.sqrt(squares + epsilon)
        return jnp.zeros_like(state[0]), (remainder / length).astype(bf16), state[2].at[KRYLOV].set(length)

    state = (cancelled, new_vector, projections)
    return lax.while_loop(lambda state: state[0][0] == 1, summed_again, state)[1:]


def solution(mesh):
    return jax.shard_map(
        per_device,
        mesh=mesh,
        in_specs=(
            P(("pitch", "span"), None, None),
            P(("pitch", "span"), None),
            P(("pitch", "span"), None),
            P(("pitch", "span"), None),
            P(None, ("pitch", "span"), None),
        ),
        out_specs=(P(("pitch", "span"), None), P()),
        check_vma=False,
    )
```

time: 78.8 us -> 69.1 us (0.88)
  blocking collectives: 32.5 us -> 24.8 us
  waiting for transfers between devices: 5.98 us -> 0.83 us
  starting transfers between devices: 15.9 us -> 19.3 us
  local copies, waits for them, and re-layouts: 5.22 us -> 4.13 us
    all_to_all x1, blocking collectives: 32.5 us -> 24.8 us  [per_device(): lax.all_to_all(sums.reshape(devices, 1, LANES), ('pitch', 'span'), 0, 0)]
    ppermute x8, waiting for transfers between devices: 5.98 us -> 0.83 us  [exchange(): received[index] = lax.ppermute(outgoing[index], axis, pairs)]
    pallas_call x2 -> x4, Pallas kernels: 4.29 us -> 8.3 us  [the longest x2 6.37 us: pack(): pl.pallas_call(functools.partial(pack_kernel, indices), out_shape=[shape(...]
    ppermute x8, starting transfers between devices: 15.9 us -> 19.3 us  [exchange(): received[index] = lax.ppermute(outgoing[index], axis, pairs)]
    pallas_call x1, Pallas kernels: 10.8 us -> 7.6 us  [per_device(): pl.pallas_call(sweeps_kernel, out_shape=[shape((BLOCK, LANES), bf16)] + [...]
    unnamed x20 -> x14, local copies, waits for them, and re-layouts: 5.22 us -> 4.13 us
    pallas_call x1, Pallas kernels: 3.16 us -> 2.32 us  [per_device(): pl.pallas_call(image_kernel, out_shape=[shape((F_DEV, BLOCK), f32), shape...]
  transfers between devices with their start and end apart: 8 -> 8, of which waited for: 2 -> 1; matrix products, arithmetic and copies ran while one was open for 0% -> 0% of each run, Pallas kernels for 0% -> 5%
where the time goes in v3:
time: 69.1 us; the launch traced here: 68.8 us
  blocking collectives  24.8 us (36%)
  starting transfers between devices  19.3 us (28%)
  Pallas kernels  18.2 us (26%)
  local copies, waits for them, and re-layouts  4.13 us (6%)
  waiting for transfers between devices  0.83 us (1%)
  between operations  0.79 us (1%)
    all_to_all x1, blocking collectives, per_device(): lax.all_to_all(sums.reshape(devices, 1, LANES), ('pitch', 'span'), 0, 0)  24.8 us
    ppermute x8, starting transfers between devices, exchange(): received[index] = lax.ppermute(outgoing[index], axis, pairs)  19.3 us
    pallas_call x1, Pallas kernels, per_device(): pl.pallas_call(sweeps_kernel, out_shape=[shape((BLOCK, LANES), bf16)] + [...  7.6 us
    pallas_call x2, Pallas kernels, pack(): pl.pallas_call(functools.partial(pack_kernel, indices), out_shape=[shape(...  6.37 us
    unnamed x14, local copies, waits for them, and re-layouts  4.13 us
    pallas_call x1, Pallas kernels, per_device(): pl.pallas_call(image_kernel, out_shape=[shape((F_DEV, BLOCK), f32), shape...  2.32 us
    pallas_call x1, Pallas kernels, per_device(): pl.pallas_call(functools.partial(last_kernel, inverse_count), out_shape=[...  1.82 us
  transfers between devices with their start and end apart: 8, of which 1 were waited for; matrix products, arithmetic and copies ran while one was open for 0% of the time, Pallas kernels for 5%

profile of v3, /device:TPU:1, one launch (start us, length us, event | category | flops | bytes accessed | tf_op | source)
XLA Modules:
  0.0 68.8 jit_solution(15383486300589995798)
XLA Ops:
  0.6 0.0 copy-start.4
  0.6 0.0 copy-start.5
  0.6 3.2 %pack_span.1 = (bf16[8,208,128]{2,1,0:T(8,128)(2,1)}, bf16[8,208,128]{2,1,0:T(8,128)(2,1)}) custom-call(s32[4,8]{1,0:T(4,128)} %lists.5, bf16[64,80,880]{2,1,0:T(8,128)(2,1)} %rows.9, bf16[8,64,80]{2,1,0:T(8,128)(2,1)} %basis.9), custom_call_target="tpu_custom_call" | custom-call | tf_op jit(solution)/shard_map/pack_span/pallas_call | solution.py:175
  3.8 5.8 %collective-permute-start = (bf16[8,208,128]{2,1,0:T(8,128)(2,1)}, bf16[8,208,128]{2,1,0:T(8,128)(2,1)S(1)}, u32[]{:S(2)}, u32[]{:S(2)}) collective-permute-start(bf16[8,208,128]{2,1,0:T(8,128)(2,1)} %get-tuple-element.50), channel_id=1, source_target_pairs={{1,2},{2,1},{3,4},{4,3},{5,6},{6,5},{7,8},{8,7},{9,10},{10,9},{11,... | collective-permute-start | bytes 1277960 | tf_op jit(solution)/shard_map/ppermute | solution.py:76
  9.7 0.0 copy-start.1
  9.7 0.0 copy-start.3
  9.7 0.0 collective-permute-start.1
  9.7 3.2 %pack_pitch.1 = (bf16[8,208,128]{2,1,0:T(8,128)(2,1)}, bf16[8,208,128]{2,1,0:T(8,128)(2,1)}) custom-call(s32[4,8]{1,0:T(4,128)} %lists.5, bf16[64,80,880]{2,1,0:T(8,128)(2,1)} %rows.9, bf16[8,64,80]{2,1,0:T(8,128)(2,1)} %basis.9), custom_call_target="tpu_custom_call" | custom-call | tf_op jit(solution)/shard_map/pack_pitch/pallas_call | solution.py:175
  12.9 2.6 %collective-permute-start.2 = (bf16[8,208,128]{2,1,0:T(8,128)(2,1)}, bf16[8,208,128]{2,1,0:T(8,128)(2,1)S(1)}, u32[]{:S(2)}, u32[]{:S(2)}) collective-permute-start(bf16[8,208,128]{2,1,0:T(8,128)(2,1)} %get-tuple-element.52), channel_id=1, source_target_pairs={{16,32},{32,16},{48,64},{64,48},{80,96},{96,80},{112,128},{128,112... | collective-permute-start | bytes 1277960 | tf_op jit(solution)/shard_map/ppermute | solution.py:76
  15.5 3.5 %collective-permute-start.3 = (bf16[8,208,128]{2,1,0:T(8,128)(2,1)}, bf16[8,208,128]{2,1,0:T(8,128)(2,1)S(1)}, u32[]{:S(2)}, u32[]{:S(2)}) collective-permute-start(bf16[8,208,128]{2,1,0:T(8,128)(2,1)} %get-tuple-element.53), channel_id=1, source_target_pairs={{0,16},{16,0},{32,48},{48,32},{64,80},{80,64},{96,112},{112,96},{1... | collective-permute-start | bytes 1277960 | tf_op jit(solution)/shard_map/ppermute | solution.py:76
  19.0 0.0 copy-done.4
  19.0 0.0 copy-done.5
  19.0 0.0 copy-start
  19.0 3.6 %copy-done = bf16[64,80,880]{2,1,0:T(8,128)(2,1)S(1)} copy-done((bf16[64,80,880]{2,1,0:T(8,128)(2,1)S(1)}, bf16[64,80,880]{2,1,0:T(8,128)(2,1)}, u32[]{:S(2)}) %copy-start) | copy-done | bytes 9011224
  22.6 0.1 choose.1.chosen
  22.7 0.0 collective-permute-done.m3
  22.7 0.0 collective-permute-done.1.m2
  22.8 0.0 collective-permute-done.2.m1
  22.8 0.0 collective-permute-done.3.m0
  22.8 0.0 copy-done.1
  22.8 0.0 copy-done.3
  22.8 7.6 %sweeps.1 = (bf16[80,128]{1,0:T(8,128)(2,1)S(1)}, f32[8,128]{1,0:T(8,128)S(1)}, f32[8,128]{1,0:T(8,128)S(1)}, f32[8,128]{1,0:T(8,128)S(1)}, f32[8,128]{1,0:T(8,128)S(1)}) custom-call(bf16[64,80,880]{2,1,0:T(8,128)(2,1)S(1)} %copy-done, bf16[128,1408]{1,0:T(8,128)(2,1)S(1)} %choose.1.chosen, s32[4,8]{1,0:T(4,128)S(1)} %copy-done.3, ...), custom_call_target="tpu_custom_call" | custom-call | tf_op jit(solution)/shard_map/sweeps/pallas_call | solution.py:298
  30.4 1.2 %collective-permute-start.4 = (f32[8,128]{1,0:T(8,128)S(1)}, f32[8,128]{1,0:T(8,128)S(1)}, u32[]{:S(2)}, u32[]{:S(2)}) collective-permute-start(f32[8,128]{1,0:T(8,128)S(1)} %get-tuple-element.55), channel_id=1, source_target_pairs={{1,2},{2,1},{3,4},{4,3},{5,6},{6,5},{7,8},{8,7},{9,10},{10,9},{11,... | collective-permute-start | bytes 12296 | tf_op jit(solution)/shard_map/ppermute | solution.py:76
  31.6 0.3 collective-permute-start.5
  31.9 3.1 %collective-permute-start.6 = (f32[8,128]{1,0:T(8,128)S(1)}, f32[8,128]{1,0:T(8,128)S(1)}, u32[]{:S(2)}, u32[]{:S(2)}) collective-permute-start(f32[8,128]{1,0:T(8,128)S(1)} %get-tuple-element.57), channel_id=1, source_target_pairs={{16,32},{32,16},{48,64},{64,48},{80,96},{96,80},{112,128},{128,112... | collective-permute-start | bytes 12296 | tf_op jit(solution)/shard_map/ppermute | solution.py:76
  35.0 2.7 %collective-permute-start.7 = (f32[8,128]{1,0:T(8,128)S(1)}, f32[8,128]{1,0:T(8,128)S(1)}, u32[]{:S(2)}, u32[]{:S(2)}) collective-permute-start(f32[8,128]{1,0:T(8,128)S(1)} %get-tuple-element.58), channel_id=1, source_target_pairs={{0,16},{16,0},{32,48},{48,32},{64,80},{80,64},{96,112},{112,96},{1... | collective-permute-start | bytes 12296 | tf_op jit(solution)/shard_map/ppermute | solution.py:76
  37.7 0.0 collective-permute-done.4.g3
  37.7 0.0 collective-permute-done.5.g2
  37.7 0.0 collective-permute-done.6.g1
  37.7 0.8 %collective-permute-done.7.g0 = f32[8,128]{1,0:T(8,128)S(1)} collective-permute-done((f32[8,128]{1,0:T(8,128)S(1)}, f32[8,128]{1,0:T(8,128)S(1)}, u32[]{:S(2)}, u32[]{:S(2)}) %collective-permute-start.7) | collective-permute-done | bytes 4128 | tf_op jit(solution)/shard_map/ppermute | solution.py:76
  38.5 2.3 %image.1 = (f32[64,80]{1,0:T(8,128)S(1)}, f32[256,128]{1,0:T(8,128)S(1)}) custom-call(bf16[64,80,880]{2,1,0:T(8,128)(2,1)S(1)} %copy-done, bf16[128,1408]{1,0:T(8,128)(2,1)S(1)} %choose.1.chosen, bf16[80,128]{1,0:T(8,128)(2,1)S(1)} %get-tuple-element.54.precond, f32[8,128]{1,0:T(8,128)S(1)} %collective-permute-done.4.g3, ...), custom_call_target="tpu_custom_call" | custom-call | tf_op jit(solution)/shard_map/image/pallas_call | solution.py:308
  40.9 0.0 copy-start.2
  40.9 24.8 %all_to_all.5 = f32[256,1,128]{2,1,0:T(1,128)} all-to-all(f32[256,1,128]{2,1,0:T(1,128)S(1)} %bitcast.8), channel_id=1, replica_groups=mesh['pitch'=16,'span'=16] {'pitch','span'}, dimensions={0} | all-to-all | bytes 262144 | tf_op jit(solution)/shard_map/all_to_all | solution.py:317
  65.7 0.0 copy-done.2
  65.7 1.8 %new_vector.1 = (bf16[64,80]{1,0:T(8,128)(2,1)}, f32[9]{0:T(128)S(1)}, f32[64,80]{1,0:T(8,128)S(1)}, s32[1]{0:T(128)}) custom-call(f32[64,80]{1,0:T(8,128)} %copy-done.2, bf16[8,64,80]{2,1,0:T(8,128)(2,1)} %basis.9, f32[256,128]{1,0:T(8,128)} %bitcast.11), custom_call_target="tpu_custom_call" | custom-call | tf_op jit(solution)/shard_map/new_vector/pallas_call | solution.py:319
  67.6 0.7 while.12
  68.2 0.0 copy-start.6
  68.2 0.5 copy-done.6
Async XLA Ops:
  0.6 18.4 %copy-start.4 = (s32[64,11]{0,1:T(8,128)S(1)}, s32[64,11]{0,1:T(8,128)}, u32[]{:S(2)}) copy-start(s32[64,11]{0,1:T(8,128)} %param.10) | copy-start | bytes 8452
  0.6 18.4 %copy-start.5 = (s32[32,4]{0,1:T(4,128)S(1)}, s32[32,4]{0,1:T(4,128)}, u32[]{:S(2)}) copy-start(s32[32,4]{0,1:T(4,128)} %param.11) | copy-start | bytes 1540
  3.8 18.9 %collective-permute-start = (bf16[8,208,128]{2,1,0:T(8,128)(2,1)}, bf16[8,208,128]{2,1,0:T(8,128)(2,1)S(1)}, u32[]{:S(2)}, u32[]{:S(2)}) collective-permute-start(bf16[8,208,128]{2,1,0:T(8,128)(2,1)} %get-tuple-element.50), channel_id=1, source_target_pairs={{1,2},{2,1},{3,4},{4,3},{5,6},{6,5},{7,8},{8,7},{9,10},{10,9},{11,... | collective-permute-start | bytes 1277960 | tf_op jit(solution)/shard_map/ppermute | solution.py:76
  9.7 13.1 %copy-start.1 = (bf16[8,64,80]{2,1,0:T(8,128)(2,1)S(1)}, bf16[8,64,80]{2,1,0:T(8,128)(2,1)}, u32[]{:S(2)}) copy-start(bf16[8,64,80]{2,1,0:T(8,128)(2,1)} %basis.9) | copy-start | bytes 245764
  9.7 13.1 %copy-start.3 = (s32[4,8]{1,0:T(4,128)S(1)}, s32[4,8]{1,0:T(4,128)}, u32[]{:S(2)}) copy-start(s32[4,8]{1,0:T(4,128)} %lists.5) | copy-start | bytes 388
  9.7 13.1 %collective-permute-start.1 = (bf16[8,208,128]{2,1,0:T(8,128)(2,1)}, bf16[8,208,128]{2,1,0:T(8,128)(2,1)S(1)}, u32[]{:S(2)}, u32[]{:S(2)}) collective-permute-start(bf16[8,208,128]{2,1,0:T(8,128)(2,1)} %get-tuple-element.51), channel_id=1, source_target_pairs={{0,1},{1,0},{2,3},{3,2},{4,5},{5,4},{6,7},{7,6},{8,9},{9,8},{10,11... | collective-permute-start | bytes 1277960 | tf_op jit(solution)/shard_map/ppermute | solution.py:76
  12.9 9.9 %collective-permute-start.2 = (bf16[8,208,128]{2,1,0:T(8,128)(2,1)}, bf16[8,208,128]{2,1,0:T(8,128)(2,1)S(1)}, u32[]{:S(2)}, u32[]{:S(2)}) collective-permute-start(bf16[8,208,128]{2,1,0:T(8,128)(2,1)} %get-tuple-element.52), channel_id=1, source_target_pairs={{16,32},{32,16},{48,64},{64,48},{80,96},{96,80},{112,128},{128,112... | collective-permute-start | bytes 1277960 | tf_op jit(solution)/shard_map/ppermute | solution.py:76
  15.5 7.3 %collective-permute-start.3 = (bf16[8,208,128]{2,1,0:T(8,128)(2,1)}, bf16[8,208,128]{2,1,0:T(8,128)(2,1)S(1)}, u32[]{:S(2)}, u32[]{:S(2)}) collective-permute-start(bf16[8,208,128]{2,1,0:T(8,128)(2,1)} %get-tuple-element.53), channel_id=1, source_target_pairs={{0,16},{16,0},{32,48},{48,32},{64,80},{80,64},{96,112},{112,96},{1... | collective-permute-start | bytes 1277960 | tf_op jit(solution)/shard_map/ppermute | solution.py:76
  19.0 3.6 %copy-start = (bf16[64,80,880]{2,1,0:T(8,128)(2,1)S(1)}, bf16[64,80,880]{2,1,0:T(8,128)(2,1)}, u32[]{:S(2)}) copy-start(bf16[64,80,880]{2,1,0:T(8,128)(2,1)} %rows.9) | copy-start | bytes 27033604
  30.4 7.3 %collective-permute-start.4 = (f32[8,128]{1,0:T(8,128)S(1)}, f32[8,128]{1,0:T(8,128)S(1)}, u32[]{:S(2)}, u32[]{:S(2)}) collective-permute-start(f32[8,128]{1,0:T(8,128)S(1)} %get-tuple-element.55), channel_id=1, source_target_pairs={{1,2},{2,1},{3,4},{4,3},{5,6},{6,5},{7,8},{8,7},{9,10},{10,9},{11,... | collective-permute-start | bytes 12296 | tf_op jit(solution)/shard_map/ppermute | solution.py:76
  31.6 6.1 %collective-permute-start.5 = (f32[8,128]{1,0:T(8,128)S(1)}, f32[8,128]{1,0:T(8,128)S(1)}, u32[]{:S(2)}, u32[]{:S(2)}) collective-permute-start(f32[8,128]{1,0:T(8,128)S(1)} %get-tuple-element.56), channel_id=1, source_target_pairs={{0,1},{1,0},{2,3},{3,2},{4,5},{5,4},{6,7},{7,6},{8,9},{9,8},{10,11... | collective-permute-start | bytes 12296 | tf_op jit(solution)/shard_map/ppermute | solution.py:76
  31.9 5.8 %collective-permute-start.6 = (f32[8,128]{1,0:T(8,128)S(1)}, f32[8,128]{1,0:T(8,128)S(1)}, u32[]{:S(2)}, u32[]{:S(2)}) collective-permute-start(f32[8,128]{1,0:T(8,128)S(1)} %get-tuple-element.57), channel_id=1, source_target_pairs={{16,32},{32,16},{48,64},{64,48},{80,96},{96,80},{112,128},{128,112... | collective-permute-start | bytes 12296 | tf_op jit(solution)/shard_map/ppermute | solution.py:76
  35.0 3.6 %collective-permute-start.7 = (f32[8,128]{1,0:T(8,128)S(1)}, f32[8,128]{1,0:T(8,128)S(1)}, u32[]{:S(2)}, u32[]{:S(2)}) collective-permute-start(f32[8,128]{1,0:T(8,128)S(1)} %get-tuple-element.58), channel_id=1, source_target_pairs={{0,16},{16,0},{32,48},{48,32},{64,80},{80,64},{96,112},{112,96},{1... | collective-permute-start | bytes 12296 | tf_op jit(solution)/shard_map/ppermute | solution.py:76
  40.9 24.9 %copy-start.2 = (f32[64,80]{1,0:T(8,128)}, f32[64,80]{1,0:T(8,128)S(1)}, u32[]{:S(2)}) copy-start(f32[64,80]{1,0:T(8,128)S(1)} %get-tuple-element.59.image) | copy-start | bytes 61444
  68.2 0.5 copy-start.6

commit v4 on v3

--- a/solution.py
+++ b/solution.py
@@ -81,7 +81,14 @@
     return lax.broadcasted_iota(jnp.int32, (BLOCK, LANES), 1)
 
 
-def choose_kernel(rows, columns, margin_columns, chosen, ids):
+def choose_kernel(rows, columns, margin_columns, basis, chosen, gram, ids):
+    gram[...] = jnp.zeros(gram.shape, f32)
+    vectors = [basis[j].astype(f32) for j in range(KRYLOV)]
+    for a in range(KRYLOV):
+        for b in range(a, KRYLOV):
+            entry = jnp.sum(vectors[a] * vectors[b], axis=0, keepdims=True)
+            for row in {KRYLOV * a + b, KRYLOV * b + a}:
+                gram[row : row + 1, 0:BLOCK] = entry
     ids[...] = jnp.full(ids.shape, LANES - 1, jnp.int32)
     ids[0:SLOTS, 0:F_DEV] = columns[...]
     ids[0:GSLOTS, F_DEV : F_DEV + 4 * LIST] = margin_columns[...]
@@ -224,27 +231,22 @@
 
 
 def image_kernel(
-    rows, chosen, precond, g3, g2, g1, g0, basis, image_out, sums_out, wide, gathered, turned, sums
+    rows, chosen, precond, g0, g1, g2, g3, basis, gram, image_out, sums_out, wide, gathered, turned, sums
 ):
     wide[...] = jnp.zeros((LANES, LANES), f32)
     for ghost, (group, there) in zip((g0, g1, g2, g3), received_groups()):
         wide[pl.ds(pl.multiple_of(F_DEV + group * LIST, LIST), LIST), :] = jnp.where(there, ghost[...], 0.0)
     vector = precond[...] + wide[...].T[0:BLOCK].astype(bf16)
     fill_gathered(vector, chosen, gathered)
-    sums[...] = jnp.zeros((LANES, LANES), f32)
-    spread = [basis[j].astype(f32) for j in range(KRYLOV)]
-    for a in range(KRYLOV):
-        for b in range(a, KRYLOV):
-            entry = jnp.sum(spread[a] * spread[b], axis=0, keepdims=True)
-            for row in {GRAM + KRYLOV * a + b, GRAM + KRYLOV * b + a}:
-                sums[row : row + 1, 0:BLOCK] = entry
+    sums[0:GRAM, :] = jnp.zeros((GRAM, LANES), f32)
+    sums[GRAM:LANES, :] = gram[...]
     product = own_product(rows, gathered, turned)
     wide[0:BLOCK, :] = product
     wide[BLOCK:LANES, :] = jnp.zeros((LANES - BLOCK, LANES), f32)
     image = wide[...].T[0:F_DEV, 0:BLOCK]
     image_out[...] = image
     for j in range(KRYLOV):
-        sums[j : j + 1, 0:BLOCK] = jnp.sum(spread[j] * image, axis=0, keepdims=True)
+        sums[j : j + 1, 0:BLOCK] = jnp.sum(basis[j].astype(f32) * image, axis=0, keepdims=True)
     sums[KRYLOV : KRYLOV + 1, 0:BLOCK] = jnp.sum(image * image, axis=0, keepdims=True)
     totals = jnp.sum(sums[...], axis=1, keepdims=True)
     row = jnp.broadcast_to(totals, (LANES, LANES)).T[0:1]
@@ -285,16 +287,16 @@
     last, third = pack((3, 2), send_lists, blocks, basis)
     second, first = pack((1, 0), send_lists, blocks, basis)
     messages = exchange([first, second, third, last])
-    chosen = pl.pallas_call(
+    chosen, gram = pl.pallas_call(
         choose_kernel,
-        out_shape=shape((LANES, SLOTS * LANES), bf16),
-        in_specs=[VMEM] * 3,
-        out_specs=VMEM,
+        out_shape=[shape((LANES, SLOTS * LANES), bf16), shape((LANES - GRAM, LANES), f32)],
+        in_specs=[VMEM] * 4,
+        out_specs=[VMEM] * 2,
         scratch_shapes=[pltpu.VMEM((16, LANES), jnp.int32)],
         compiler_params=PARAMS,
         cost_estimate=pl.CostEstimate(flops=0, bytes_accessed=2**20, transcendentals=0),
         name="choose",
-    )(blocks, columns.T, margin_columns.T)
+    )(blocks, columns.T, margin_columns.T, basis)
     precond, *values = pl.pallas_call(
         sweeps_kernel,
         out_shape=[shape((BLOCK, LANES), bf16)] + [shape((LIST, LANES), f32)] * 4,
@@ -308,12 +310,12 @@
     image, sums = pl.pallas_call(
         image_kernel,
         out_shape=[shape((F_DEV, BLOCK), f32), shape((devices, LANES), f32)],
-        in_specs=[VMEM] * 8,
+        in_specs=[VMEM] * 9,
         out_specs=[VMEM] * 2,
         scratch_shapes=[square, gathered, turned, square],
         compiler_params=PARAMS,
         name="image",
-    )(blocks, chosen, precond, *ghosts[::-1], basis)
+    )(blocks, chosen, precond, *ghosts, basis, gram)
     sums = lax.all_to_all(sums.reshape(devices, 1, LANES), ("pitch", "span"), 0, 0)
     inverse_count = 1.0 / (devices * F_DEV * BLOCK)
     new_vector, projections, remainder, cancelled = pl.pallas_call(

time: 69.1 us -> 68.5 us (level)
  waiting for transfers between devices: 0.83 us -> 4.99 us
  starting transfers between devices: 19.3 us -> 16.2 us
  blocking collectives: 24.8 us -> 23.1 us
    ppermute x8, waiting for transfers between devices: 0.83 us -> 4.99 us  [exchange(): received[index] = lax.ppermute(outgoing[index], axis, pairs)]
    ppermute x8, starting transfers between devices: 19.3 us -> 16.2 us  [exchange(): received[index] = lax.ppermute(outgoing[index], axis, pairs)]
    all_to_all x1, blocking collectives: 24.8 us -> 23.1 us  [per_device(): lax.all_to_all(sums.reshape(devices, 1, LANES), ('pitch', 'span'), 0, 0)]
  transfers between devices with their start and end apart: 8 -> 8, of which waited for: 1 -> 2; matrix products, arithmetic and copies ran while one was open for 0% -> 0% of each run, Pallas kernels for 5% -> 5%
where the time goes in v4:
time: 68.5 us; the launch traced here: 68.1 us
  blocking collectives  23.1 us (34%)
  Pallas kernels  18.2 us (27%)
  starting transfers between devices  16.2 us (24%)
  waiting for transfers between devices  4.99 us (7%)
  local copies, waits for them, and re-layouts  4.13 us (6%)
  between operations  0.79 us (1%)
    all_to_all x1, blocking collectives, per_device(): lax.all_to_all(sums.reshape(devices, 1, LANES), ('pitch', 'span'), 0, 0)  23.1 us
    ppermute x8, starting transfers between devices, exchange(): received[index] = lax.ppermute(outgoing[index], axis, pairs)  16.2 us
    pallas_call x1, Pallas kernels, per_device(): pl.pallas_call(sweeps_kernel, out_shape=[shape((BLOCK, LANES), bf16)] + [...  7.59 us
    pallas_call x2, Pallas kernels, pack(): pl.pallas_call(functools.partial(pack_kernel, indices), out_shape=[shape(...  6.36 us
    ppermute x8, waiting for transfers between devices, exchange(): received[index] = lax.ppermute(outgoing[index], axis, pairs)  4.99 us
    unnamed x14, local copies, waits for them, and re-layouts  4.13 us
    pallas_call x1, Pallas kernels, per_device(): pl.pallas_call(image_kernel, out_shape=[shape((F_DEV, BLOCK), f32), shape...  2.21 us
    pallas_call x1, Pallas kernels, per_device(): pl.pallas_call(functools.partial(last_kernel, inverse_count), out_shape=[...  1.82 us
  transfers between devices with their start and end apart: 8, of which 2 were waited for; matrix products, arithmetic and copies ran while one was open for 0% of the time, Pallas kernels for 5%

profile of v4, /device:TPU:1, one launch (start us, length us, event | category | flops | bytes accessed | tf_op | source)
XLA Modules:
  0.0 68.1 jit_solution(11868263400623607361)
XLA Ops:
  0.6 0.0 copy-start.1
  0.6 0.0 copy-start.5
  0.7 0.0 copy-start.4
  0.7 3.2 %pack_span.1 = (bf16[8,208,128]{2,1,0:T(8,128)(2,1)}, bf16[8,208,128]{2,1,0:T(8,128)(2,1)}) custom-call(s32[4,8]{1,0:T(4,128)} %lists.5, bf16[64,80,880]{2,1,0:T(8,128)(2,1)} %rows.9, bf16[8,64,80]{2,1,0:T(8,128)(2,1)} %basis.11), custom_call_target="tpu_custom_call" | custom-call | tf_op jit(solution)/shard_map/pack_span/pallas_call | solution.py:182
  3.8 5.8 %collective-permute-start = (bf16[8,208,128]{2,1,0:T(8,128)(2,1)}, bf16[8,208,128]{2,1,0:T(8,128)(2,1)S(1)}, u32[]{:S(2)}, u32[]{:S(2)}) collective-permute-start(bf16[8,208,128]{2,1,0:T(8,128)(2,1)} %get-tuple-element.53), channel_id=1, source_target_pairs={{1,2},{2,1},{3,4},{4,3},{5,6},{6,5},{7,8},{8,7},{9,10},{10,9},{11,... | collective-permute-start | bytes 1277960 | tf_op jit(solution)/shard_map/ppermute | solution.py:76
  9.7 0.0 copy-start.3
  9.7 0.0 collective-permute-start.1
  9.7 3.2 %pack_pitch.1 = (bf16[8,208,128]{2,1,0:T(8,128)(2,1)}, bf16[8,208,128]{2,1,0:T(8,128)(2,1)}) custom-call(s32[4,8]{1,0:T(4,128)} %lists.5, bf16[64,80,880]{2,1,0:T(8,128)(2,1)} %rows.9, bf16[8,64,80]{2,1,0:T(8,128)(2,1)} %basis.11), custom_call_target="tpu_custom_call" | custom-call | tf_op jit(solution)/shard_map/pack_pitch/pallas_call | solution.py:182
  12.9 2.6 %collective-permute-start.2 = (bf16[8,208,128]{2,1,0:T(8,128)(2,1)}, bf16[8,208,128]{2,1,0:T(8,128)(2,1)S(1)}, u32[]{:S(2)}, u32[]{:S(2)}) collective-permute-start(bf16[8,208,128]{2,1,0:T(8,128)(2,1)} %get-tuple-element.55), channel_id=1, source_target_pairs={{16,32},{32,16},{48,64},{64,48},{80,96},{96,80},{112,128},{128,112... | collective-permute-start | bytes 1277960 | tf_op jit(solution)/shard_map/ppermute | solution.py:76
  15.5 3.5 %collective-permute-start.3 = (bf16[8,208,128]{2,1,0:T(8,128)(2,1)}, bf16[8,208,128]{2,1,0:T(8,128)(2,1)S(1)}, u32[]{:S(2)}, u32[]{:S(2)}) collective-permute-start(bf16[8,208,128]{2,1,0:T(8,128)(2,1)} %get-tuple-element.56), channel_id=1, source_target_pairs={{0,16},{16,0},{32,48},{48,32},{64,80},{80,64},{96,112},{112,96},{1... | collective-permute-start | bytes 1277960 | tf_op jit(solution)/shard_map/ppermute | solution.py:76
  18.9 0.0 copy-done.1
  19.0 0.0 copy-done.5
  19.0 0.0 copy-done.4
  19.0 0.0 copy-start
  19.0 3.6 %copy-done = bf16[64,80,880]{2,1,0:T(8,128)(2,1)S(1)} copy-done((bf16[64,80,880]{2,1,0:T(8,128)(2,1)S(1)}, bf16[64,80,880]{2,1,0:T(8,128)(2,1)}, u32[]{:S(2)}) %copy-start) | copy-done | bytes 9011224
  22.6 0.2 choose.1
  22.8 0.0 collective-permute-done.m3
  22.8 0.0 collective-permute-done.1.m2
  22.8 0.0 collective-permute-done.2.m1
  22.8 0.0 collective-permute-done.3.m0
  22.8 0.0 copy-done.3
  22.8 7.6 %sweeps.1 = (bf16[80,128]{1,0:T(8,128)(2,1)S(1)}, f32[8,128]{1,0:T(8,128)S(1)}, f32[8,128]{1,0:T(8,128)S(1)}, f32[8,128]{1,0:T(8,128)S(1)}, f32[8,128]{1,0:T(8,128)S(1)}) custom-call(bf16[64,80,880]{2,1,0:T(8,128)(2,1)S(1)} %copy-done, bf16[128,1408]{1,0:T(8,128)(2,1)S(1)} %get-tuple-element.52.chosen, s32[4,8]{1,0:T(4,128)S(1)} %copy-done.3, ...), custom_call_target="tpu_custom_call" | custom-call | tf_op jit(solution)/shard_map/sweeps/pallas_call | solution.py:300
  30.4 2.2 %collective-permute-start.4 = (f32[8,128]{1,0:T(8,128)S(1)}, f32[8,128]{1,0:T(8,128)S(1)}, u32[]{:S(2)}, u32[]{:S(2)}) collective-permute-start(f32[8,128]{1,0:T(8,128)S(1)} %get-tuple-element.58), channel_id=1, source_target_pairs={{0,16},{16,0},{32,48},{48,32},{64,80},{80,64},{96,112},{112,96},{1... | collective-permute-start | bytes 12296 | tf_op jit(solution)/shard_map/ppermute | solution.py:76
  32.7 0.0 collective-permute-start.5
  32.7 1.3 %collective-permute-start.6 = (f32[8,128]{1,0:T(8,128)S(1)}, f32[8,128]{1,0:T(8,128)S(1)}, u32[]{:S(2)}, u32[]{:S(2)}) collective-permute-start(f32[8,128]{1,0:T(8,128)S(1)} %get-tuple-element.60), channel_id=1, source_target_pairs={{0,1},{1,0},{2,3},{3,2},{4,5},{5,4},{6,7},{7,6},{8,9},{9,8},{10,11... | collective-permute-start | bytes 12296 | tf_op jit(solution)/shard_map/ppermute | solution.py:76
  34.0 0.8 %collective-permute-start.7 = (f32[8,128]{1,0:T(8,128)S(1)}, f32[8,128]{1,0:T(8,128)S(1)}, u32[]{:S(2)}, u32[]{:S(2)}) collective-permute-start(f32[8,128]{1,0:T(8,128)S(1)} %get-tuple-element.61), channel_id=1, source_target_pairs={{1,2},{2,1},{3,4},{4,3},{5,6},{6,5},{7,8},{8,7},{9,10},{10,9},{11,... | collective-permute-start | bytes 12296 | tf_op jit(solution)/shard_map/ppermute | solution.py:76
  34.8 0.0 collective-permute-done.4.g0
  34.8 0.9 %collective-permute-done.5.g1 = f32[8,128]{1,0:T(8,128)S(1)} collective-permute-done((f32[8,128]{1,0:T(8,128)S(1)}, f32[8,128]{1,0:T(8,128)S(1)}, u32[]{:S(2)}, u32[]{:S(2)}) %collective-permute-start.5) | collective-permute-done | bytes 4128 | tf_op jit(solution)/shard_map/ppermute | solution.py:76
  35.7 0.0 collective-permute-done.6.g2
  35.7 4.1 %collective-permute-done.7.g3 = f32[8,128]{1,0:T(8,128)S(1)} collective-permute-done((f32[8,128]{1,0:T(8,128)S(1)}, f32[8,128]{1,0:T(8,128)S(1)}, u32[]{:S(2)}, u32[]{:S(2)}) %collective-permute-start.7) | collective-permute-done | bytes 4128 | tf_op jit(solution)/shard_map/ppermute | solution.py:76
  39.8 2.2 %image.1 = (f32[64,80]{1,0:T(8,128)S(1)}, f32[256,128]{1,0:T(8,128)S(1)}) custom-call(bf16[64,80,880]{2,1,0:T(8,128)(2,1)S(1)} %copy-done, bf16[128,1408]{1,0:T(8,128)(2,1)S(1)} %get-tuple-element.52.chosen, bf16[80,128]{1,0:T(8,128)(2,1)S(1)} %get-tuple-element.57.precond, f32[8,128]{1,0:T(8,128)S(1)} %collective-permute-done.4.g0, ...), custom_call_target="tpu_custom_call" | custom-call | tf_op jit(solution)/shard_map/image/pallas_call | solution.py:310
  42.0 0.0 copy-start.2
  42.0 23.1 %all_to_all.5 = f32[256,1,128]{2,1,0:T(1,128)} all-to-all(f32[256,1,128]{2,1,0:T(1,128)S(1)} %bitcast.8), channel_id=1, replica_groups=mesh['pitch'=16,'span'=16] {'pitch','span'}, dimensions={0} | all-to-all | bytes 262144 | tf_op jit(solution)/shard_map/all_to_all | solution.py:319
  65.1 0.0 copy-done.2
  65.1 1.8 %new_vector.1 = (bf16[64,80]{1,0:T(8,128)(2,1)}, f32[9]{0:T(128)S(1)}, f32[64,80]{1,0:T(8,128)S(1)}, s32[1]{0:T(128)}) custom-call(f32[64,80]{1,0:T(8,128)} %copy-done.2, bf16[8,64,80]{2,1,0:T(8,128)(2,1)} %basis.11, f32[256,128]{1,0:T(8,128)} %bitcast.11), custom_call_target="tpu_custom_call" | custom-call | tf_op jit(solution)/shard_map/new_vector/pallas_call | solution.py:321
  66.9 0.7 while.12
  67.6 0.0 copy-start.6
  67.6 0.5 copy-done.6
Async XLA Ops:
  0.6 18.3 %copy-start.1 = (bf16[8,64,80]{2,1,0:T(8,128)(2,1)S(1)}, bf16[8,64,80]{2,1,0:T(8,128)(2,1)}, u32[]{:S(2)}) copy-start(bf16[8,64,80]{2,1,0:T(8,128)(2,1)} %basis.11) | copy-start | bytes 245764
  0.6 18.3 %copy-start.5 = (s32[32,4]{0,1:T(4,128)S(1)}, s32[32,4]{0,1:T(4,128)}, u32[]{:S(2)}) copy-start(s32[32,4]{0,1:T(4,128)} %param.11) | copy-start | bytes 1540
  0.7 18.3 %copy-start.4 = (s32[64,11]{0,1:T(8,128)S(1)}, s32[64,11]{0,1:T(8,128)}, u32[]{:S(2)}) copy-start(s32[64,11]{0,1:T(8,128)} %param.10) | copy-start | bytes 8452
  3.8 19.0 %collective-permute-start = (bf16[8,208,128]{2,1,0:T(8,128)(2,1)}, bf16[8,208,128]{2,1,0:T(8,128)(2,1)S(1)}, u32[]{:S(2)}, u32[]{:S(2)}) collective-permute-start(bf16[8,208,128]{2,1,0:T(8,128)(2,1)} %get-tuple-element.53), channel_id=1, source_target_pairs={{1,2},{2,1},{3,4},{4,3},{5,6},{6,5},{7,8},{8,7},{9,10},{10,9},{11,... | collective-permute-start | bytes 1277960 | tf_op jit(solution)/shard_map/ppermute | solution.py:76
  9.7 13.2 %copy-start.3 = (s32[4,8]{1,0:T(4,128)S(1)}, s32[4,8]{1,0:T(4,128)}, u32[]{:S(2)}) copy-start(s32[4,8]{1,0:T(4,128)} %lists.5) | copy-start | bytes 388
  9.7 13.1 %collective-permute-start.1 = (bf16[8,208,128]{2,1,0:T(8,128)(2,1)}, bf16[8,208,128]{2,1,0:T(8,128)(2,1)S(1)}, u32[]{:S(2)}, u32[]{:S(2)}) collective-permute-start(bf16[8,208,128]{2,1,0:T(8,128)(2,1)} %get-tuple-element.54), channel_id=1, source_target_pairs={{0,1},{1,0},{2,3},{3,2},{4,5},{5,4},{6,7},{7,6},{8,9},{9,8},{10,11... | collective-permute-start | bytes 1277960 | tf_op jit(solution)/shard_map/ppermute | solution.py:76
  12.9 9.9 %collective-permute-start.2 = (bf16[8,208,128]{2,1,0:T(8,128)(2,1)}, bf16[8,208,128]{2,1,0:T(8,128)(2,1)S(1)}, u32[]{:S(2)}, u32[]{:S(2)}) collective-permute-start(bf16[8,208,128]{2,1,0:T(8,128)(2,1)} %get-tuple-element.55), channel_id=1, source_target_pairs={{16,32},{32,16},{48,64},{64,48},{80,96},{96,80},{112,128},{128,112... | collective-permute-start | bytes 1277960 | tf_op jit(solution)/shard_map/ppermute | solution.py:76
  15.5 7.4 %collective-permute-start.3 = (bf16[8,208,128]{2,1,0:T(8,128)(2,1)}, bf16[8,208,128]{2,1,0:T(8,128)(2,1)S(1)}, u32[]{:S(2)}, u32[]{:S(2)}) collective-permute-start(bf16[8,208,128]{2,1,0:T(8,128)(2,1)} %get-tuple-element.56), channel_id=1, source_target_pairs={{0,16},{16,0},{32,48},{48,32},{64,80},{80,64},{96,112},{112,96},{1... | collective-permute-start | bytes 1277960 | tf_op jit(solution)/shard_map/ppermute | solution.py:76
  19.0 3.6 %copy-start = (bf16[64,80,880]{2,1,0:T(8,128)(2,1)S(1)}, bf16[64,80,880]{2,1,0:T(8,128)(2,1)}, u32[]{:S(2)}) copy-start(bf16[64,80,880]{2,1,0:T(8,128)(2,1)} %rows.9) | copy-start | bytes 27033604
  30.4 4.3 %collective-permute-start.4 = (f32[8,128]{1,0:T(8,128)S(1)}, f32[8,128]{1,0:T(8,128)S(1)}, u32[]{:S(2)}, u32[]{:S(2)}) collective-permute-start(f32[8,128]{1,0:T(8,128)S(1)} %get-tuple-element.58), channel_id=1, source_target_pairs={{0,16},{16,0},{32,48},{48,32},{64,80},{80,64},{96,112},{112,96},{1... | collective-permute-start | bytes 12296 | tf_op jit(solution)/shard_map/ppermute | solution.py:76
  32.7 3.0 %collective-permute-start.5 = (f32[8,128]{1,0:T(8,128)S(1)}, f32[8,128]{1,0:T(8,128)S(1)}, u32[]{:S(2)}, u32[]{:S(2)}) collective-permute-start(f32[8,128]{1,0:T(8,128)S(1)} %get-tuple-element.59), channel_id=1, source_target_pairs={{16,32},{32,16},{48,64},{64,48},{80,96},{96,80},{112,128},{128,112... | collective-permute-start | bytes 12296 | tf_op jit(solution)/shard_map/ppermute | solution.py:76
  32.7 3.0 %collective-permute-start.6 = (f32[8,128]{1,0:T(8,128)S(1)}, f32[8,128]{1,0:T(8,128)S(1)}, u32[]{:S(2)}, u32[]{:S(2)}) collective-permute-start(f32[8,128]{1,0:T(8,128)S(1)} %get-tuple-element.60), channel_id=1, source_target_pairs={{0,1},{1,0},{2,3},{3,2},{4,5},{5,4},{6,7},{7,6},{8,9},{9,8},{10,11... | collective-permute-start | bytes 12296 | tf_op jit(solution)/shard_map/ppermute | solution.py:76
  34.0 5.8 %collective-permute-start.7 = (f32[8,128]{1,0:T(8,128)S(1)}, f32[8,128]{1,0:T(8,128)S(1)}, u32[]{:S(2)}, u32[]{:S(2)}) collective-permute-start(f32[8,128]{1,0:T(8,128)S(1)} %get-tuple-element.61), channel_id=1, source_target_pairs={{1,2},{2,1},{3,4},{4,3},{5,6},{6,5},{7,8},{8,7},{9,10},{10,9},{11,... | collective-permute-start | bytes 12296 | tf_op jit(solution)/shard_map/ppermute | solution.py:76
  42.0 23.1 %copy-start.2 = (f32[64,80]{1,0:T(8,128)}, f32[64,80]{1,0:T(8,128)S(1)}, u32[]{:S(2)}) copy-start(f32[64,80]{1,0:T(8,128)S(1)} %get-tuple-element.63.image) | copy-start | bytes 61444
  67.6 0.5 copy-start.6

commit v5 on v4

--- a/solution.py
+++ b/solution.py
@@ -22,7 +22,7 @@
 GUARD = 2.0**-11
 KTILES = ((0, 256), (256, 512), (512, 768), (768, 880))
 REST = 768
-SPLIT = 24
+SPLIT = 22
 
 center_value = 1.0
 half_width = 0.5

time: 68.5 us -> 68.3 us (level)
  no operation moved by 1% of the time
where the time goes in v5:
time: 68.3 us; the launch traced here: 68 us
  blocking collectives  23.1 us (34%)
  Pallas kernels  18 us (26%)
  starting transfers between devices  16.3 us (24%)
  waiting for transfers between devices  5 us (7%)
  local copies, waits for them, and re-layouts  4.13 us (6%)
  between operations  0.79 us (1%)
    all_to_all x1, blocking collectives, per_device(): lax.all_to_all(sums.reshape(devices, 1, LANES), ('pitch', 'span'), 0, 0)  23.1 us
    ppermute x8, starting transfers between devices, exchange(): received[index] = lax.ppermute(outgoing[index], axis, pairs)  16.3 us
    pallas_call x1, Pallas kernels, per_device(): pl.pallas_call(sweeps_kernel, out_shape=[shape((BLOCK, LANES), bf16)] + [...  7.42 us
    pallas_call x2, Pallas kernels, pack(): pl.pallas_call(functools.partial(pack_kernel, indices), out_shape=[shape(...  6.36 us
    ppermute x8, waiting for transfers between devices, exchange(): received[index] = lax.ppermute(outgoing[index], axis, pairs)  5 us
    unnamed x14, local copies, waits for them, and re-layouts  4.13 us
    pallas_call x1, Pallas kernels, per_device(): pl.pallas_call(image_kernel, out_shape=[shape((F_DEV, BLOCK), f32), shape...  2.22 us
    pallas_call x1, Pallas kernels, per_device(): pl.pallas_call(functools.partial(last_kernel, inverse_count), out_shape=[...  1.82 us
  transfers between devices with their start and end apart: 8, of which 2 were waited for; matrix products, arithmetic and copies ran while one was open for 0% of the time, Pallas kernels for 5%

profile of v5, /device:TPU:1, one launch (start us, length us, event | category | flops | bytes accessed | tf_op | source)
XLA Modules:
  0.0 68.0 jit_solution(13044023762787714771)
XLA Ops:
  0.6 0.0 copy-start.1
  0.6 0.0 copy-start.5
  0.7 0.0 copy-start.4
  0.7 3.2 %pack_span.1 = (bf16[8,208,128]{2,1,0:T(8,128)(2,1)}, bf16[8,208,128]{2,1,0:T(8,128)(2,1)}) custom-call(s32[4,8]{1,0:T(4,128)} %lists.5, bf16[64,80,880]{2,1,0:T(8,128)(2,1)} %rows.9, bf16[8,64,80]{2,1,0:T(8,128)(2,1)} %basis.11), custom_call_target="tpu_custom_call" | custom-call | tf_op jit(solution)/shard_map/pack_span/pallas_call | solution.py:182
  3.8 5.8 %collective-permute-start = (bf16[8,208,128]{2,1,0:T(8,128)(2,1)}, bf16[8,208,128]{2,1,0:T(8,128)(2,1)S(1)}, u32[]{:S(2)}, u32[]{:S(2)}) collective-permute-start(bf16[8,208,128]{2,1,0:T(8,128)(2,1)} %get-tuple-element.53), channel_id=1, source_target_pairs={{1,2},{2,1},{3,4},{4,3},{5,6},{6,5},{7,8},{8,7},{9,10},{10,9},{11,... | collective-permute-start | bytes 1277960 | tf_op jit(solution)/shard_map/ppermute | solution.py:76
  9.7 0.0 copy-start.3
  9.7 0.0 collective-permute-start.1
  9.7 3.2 %pack_pitch.1 = (bf16[8,208,128]{2,1,0:T(8,128)(2,1)}, bf16[8,208,128]{2,1,0:T(8,128)(2,1)}) custom-call(s32[4,8]{1,0:T(4,128)} %lists.5, bf16[64,80,880]{2,1,0:T(8,128)(2,1)} %rows.9, bf16[8,64,80]{2,1,0:T(8,128)(2,1)} %basis.11), custom_call_target="tpu_custom_call" | custom-call | tf_op jit(solution)/shard_map/pack_pitch/pallas_call | solution.py:182
  12.9 2.6 %collective-permute-start.2 = (bf16[8,208,128]{2,1,0:T(8,128)(2,1)}, bf16[8,208,128]{2,1,0:T(8,128)(2,1)S(1)}, u32[]{:S(2)}, u32[]{:S(2)}) collective-permute-start(bf16[8,208,128]{2,1,0:T(8,128)(2,1)} %get-tuple-element.55), channel_id=1, source_target_pairs={{16,32},{32,16},{48,64},{64,48},{80,96},{96,80},{112,128},{128,112... | collective-permute-start | bytes 1277960 | tf_op jit(solution)/shard_map/ppermute | solution.py:76
  15.5 3.5 %collective-permute-start.3 = (bf16[8,208,128]{2,1,0:T(8,128)(2,1)}, bf16[8,208,128]{2,1,0:T(8,128)(2,1)S(1)}, u32[]{:S(2)}, u32[]{:S(2)}) collective-permute-start(bf16[8,208,128]{2,1,0:T(8,128)(2,1)} %get-tuple-element.56), channel_id=1, source_target_pairs={{0,16},{16,0},{32,48},{48,32},{64,80},{80,64},{96,112},{112,96},{1... | collective-permute-start | bytes 1277960 | tf_op jit(solution)/shard_map/ppermute | solution.py:76
  19.0 0.0 copy-done.1
  19.0 0.0 copy-done.5
  19.0 0.0 copy-done.4
  19.0 0.0 copy-start
  19.0 3.6 %copy-done = bf16[64,80,880]{2,1,0:T(8,128)(2,1)S(1)} copy-done((bf16[64,80,880]{2,1,0:T(8,128)(2,1)S(1)}, bf16[64,80,880]{2,1,0:T(8,128)(2,1)}, u32[]{:S(2)}) %copy-start) | copy-done | bytes 9011224
  22.6 0.2 choose.1
  22.8 0.0 collective-permute-done.m3
  22.8 0.0 collective-permute-done.1.m2
  22.8 0.0 collective-permute-done.2.m1
  22.8 0.0 collective-permute-done.3.m0
  22.9 0.0 copy-done.3
  22.9 7.4 %sweeps.1 = (bf16[80,128]{1,0:T(8,128)(2,1)S(1)}, f32[8,128]{1,0:T(8,128)S(1)}, f32[8,128]{1,0:T(8,128)S(1)}, f32[8,128]{1,0:T(8,128)S(1)}, f32[8,128]{1,0:T(8,128)S(1)}) custom-call(bf16[64,80,880]{2,1,0:T(8,128)(2,1)S(1)} %copy-done, bf16[128,1408]{1,0:T(8,128)(2,1)S(1)} %get-tuple-element.52.chosen, s32[4,8]{1,0:T(4,128)S(1)} %copy-done.3, ...), custom_call_target="tpu_custom_call" | custom-call | tf_op jit(solution)/shard_map/sweeps/pallas_call | solution.py:300
  30.3 2.2 %collective-permute-start.4 = (f32[8,128]{1,0:T(8,128)S(1)}, f32[8,128]{1,0:T(8,128)S(1)}, u32[]{:S(2)}, u32[]{:S(2)}) collective-permute-start(f32[8,128]{1,0:T(8,128)S(1)} %get-tuple-element.58), channel_id=1, source_target_pairs={{0,16},{16,0},{32,48},{48,32},{64,80},{80,64},{96,112},{112,96},{1... | collective-permute-start | bytes 12296 | tf_op jit(solution)/shard_map/ppermute | solution.py:76
  32.5 0.0 collective-permute-start.5
  32.5 1.3 %collective-permute-start.6 = (f32[8,128]{1,0:T(8,128)S(1)}, f32[8,128]{1,0:T(8,128)S(1)}, u32[]{:S(2)}, u32[]{:S(2)}) collective-permute-start(f32[8,128]{1,0:T(8,128)S(1)} %get-tuple-element.60), channel_id=1, source_target_pairs={{0,1},{1,0},{2,3},{3,2},{4,5},{5,4},{6,7},{7,6},{8,9},{9,8},{10,11... | collective-permute-start | bytes 12296 | tf_op jit(solution)/shard_map/ppermute | solution.py:76
  33.8 0.8 %collective-permute-start.7 = (f32[8,128]{1,0:T(8,128)S(1)}, f32[8,128]{1,0:T(8,128)S(1)}, u32[]{:S(2)}, u32[]{:S(2)}) collective-permute-start(f32[8,128]{1,0:T(8,128)S(1)} %get-tuple-element.61), channel_id=1, source_target_pairs={{1,2},{2,1},{3,4},{4,3},{5,6},{6,5},{7,8},{8,7},{9,10},{10,9},{11,... | collective-permute-start | bytes 12296 | tf_op jit(solution)/shard_map/ppermute | solution.py:76
  34.6 0.0 collective-permute-done.4.g0
  34.6 0.9 %collective-permute-done.5.g1 = f32[8,128]{1,0:T(8,128)S(1)} collective-permute-done((f32[8,128]{1,0:T(8,128)S(1)}, f32[8,128]{1,0:T(8,128)S(1)}, u32[]{:S(2)}, u32[]{:S(2)}) %collective-permute-start.5) | collective-permute-done | bytes 4128 | tf_op jit(solution)/shard_map/ppermute | solution.py:76
  35.5 0.0 collective-permute-done.6.g2
  35.5 4.1 %collective-permute-done.7.g3 = f32[8,128]{1,0:T(8,128)S(1)} collective-permute-done((f32[8,128]{1,0:T(8,128)S(1)}, f32[8,128]{1,0:T(8,128)S(1)}, u32[]{:S(2)}, u32[]{:S(2)}) %collective-permute-start.7) | collective-permute-done | bytes 4128 | tf_op jit(solution)/shard_map/ppermute | solution.py:76
  39.6 2.2 %image.1 = (f32[64,80]{1,0:T(8,128)S(1)}, f32[256,128]{1,0:T(8,128)S(1)}) custom-call(bf16[64,80,880]{2,1,0:T(8,128)(2,1)S(1)} %copy-done, bf16[128,1408]{1,0:T(8,128)(2,1)S(1)} %get-tuple-element.52.chosen, bf16[80,128]{1,0:T(8,128)(2,1)S(1)} %get-tuple-element.57.precond, f32[8,128]{1,0:T(8,128)S(1)} %collective-permute-done.4.g0, ...), custom_call_target="tpu_custom_call" | custom-call | tf_op jit(solution)/shard_map/image/pallas_call | solution.py:310
  41.9 0.0 copy-start.2
  41.9 23.1 %all_to_all.5 = f32[256,1,128]{2,1,0:T(1,128)} all-to-all(f32[256,1,128]{2,1,0:T(1,128)S(1)} %bitcast.8), channel_id=1, replica_groups=mesh['pitch'=16,'span'=16] {'pitch','span'}, dimensions={0} | all-to-all | bytes 262144 | tf_op jit(solution)/shard_map/all_to_all | solution.py:319
  65.0 0.0 copy-done.2
  65.0 1.8 %new_vector.1 = (bf16[64,80]{1,0:T(8,128)(2,1)}, f32[9]{0:T(128)S(1)}, f32[64,80]{1,0:T(8,128)S(1)}, s32[1]{0:T(128)}) custom-call(f32[64,80]{1,0:T(8,128)} %copy-done.2, bf16[8,64,80]{2,1,0:T(8,128)(2,1)} %basis.11, f32[256,128]{1,0:T(8,128)} %bitcast.11), custom_call_target="tpu_custom_call" | custom-call | tf_op jit(solution)/shard_map/new_vector/pallas_call | solution.py:321
  66.8 0.7 while.12
  67.5 0.0 copy-start.6
  67.5 0.5 copy-done.6
Async XLA Ops:
  0.6 18.3 %copy-start.1 = (bf16[8,64,80]{2,1,0:T(8,128)(2,1)S(1)}, bf16[8,64,80]{2,1,0:T(8,128)(2,1)}, u32[]{:S(2)}) copy-start(bf16[8,64,80]{2,1,0:T(8,128)(2,1)} %basis.11) | copy-start | bytes 245764
  0.6 18.3 %copy-start.5 = (s32[32,4]{0,1:T(4,128)S(1)}, s32[32,4]{0,1:T(4,128)}, u32[]{:S(2)}) copy-start(s32[32,4]{0,1:T(4,128)} %param.11) | copy-start | bytes 1540
  0.7 18.3 %copy-start.4 = (s32[64,11]{0,1:T(8,128)S(1)}, s32[64,11]{0,1:T(8,128)}, u32[]{:S(2)}) copy-start(s32[64,11]{0,1:T(8,128)} %param.10) | copy-start | bytes 8452
  3.8 19.0 %collective-permute-start = (bf16[8,208,128]{2,1,0:T(8,128)(2,1)}, bf16[8,208,128]{2,1,0:T(8,128)(2,1)S(1)}, u32[]{:S(2)}, u32[]{:S(2)}) collective-permute-start(bf16[8,208,128]{2,1,0:T(8,128)(2,1)} %get-tuple-element.53), channel_id=1, source_target_pairs={{1,2},{2,1},{3,4},{4,3},{5,6},{6,5},{7,8},{8,7},{9,10},{10,9},{11,... | collective-permute-start | bytes 1277960 | tf_op jit(solution)/shard_map/ppermute | solution.py:76
  9.7 13.2 %copy-start.3 = (s32[4,8]{1,0:T(4,128)S(1)}, s32[4,8]{1,0:T(4,128)}, u32[]{:S(2)}) copy-start(s32[4,8]{1,0:T(4,128)} %lists.5) | copy-start | bytes 388
  9.7 13.1 %collective-permute-start.1 = (bf16[8,208,128]{2,1,0:T(8,128)(2,1)}, bf16[8,208,128]{2,1,0:T(8,128)(2,1)S(1)}, u32[]{:S(2)}, u32[]{:S(2)}) collective-permute-start(bf16[8,208,128]{2,1,0:T(8,128)(2,1)} %get-tuple-element.54), channel_id=1, source_target_pairs={{0,1},{1,0},{2,3},{3,2},{4,5},{5,4},{6,7},{7,6},{8,9},{9,8},{10,11... | collective-permute-start | bytes 1277960 | tf_op jit(solution)/shard_map/ppermute | solution.py:76
  12.9 9.9 %collective-permute-start.2 = (bf16[8,208,128]{2,1,0:T(8,128)(2,1)}, bf16[8,208,128]{2,1,0:T(8,128)(2,1)S(1)}, u32[]{:S(2)}, u32[]{:S(2)}) collective-permute-start(bf16[8,208,128]{2,1,0:T(8,128)(2,1)} %get-tuple-element.55), channel_id=1, source_target_pairs={{16,32},{32,16},{48,64},{64,48},{80,96},{96,80},{112,128},{128,112... | collective-permute-start | bytes 1277960 | tf_op jit(solution)/shard_map/ppermute | solution.py:76
  15.5 7.4 %collective-permute-start.3 = (bf16[8,208,128]{2,1,0:T(8,128)(2,1)}, bf16[8,208,128]{2,1,0:T(8,128)(2,1)S(1)}, u32[]{:S(2)}, u32[]{:S(2)}) collective-permute-start(bf16[8,208,128]{2,1,0:T(8,128)(2,1)} %get-tuple-element.56), channel_id=1, source_target_pairs={{0,16},{16,0},{32,48},{48,32},{64,80},{80,64},{96,112},{112,96},{1... | collective-permute-start | bytes 1277960 | tf_op jit(solution)/shard_map/ppermute | solution.py:76
  19.0 3.6 %copy-start = (bf16[64,80,880]{2,1,0:T(8,128)(2,1)S(1)}, bf16[64,80,880]{2,1,0:T(8,128)(2,1)}, u32[]{:S(2)}) copy-start(bf16[64,80,880]{2,1,0:T(8,128)(2,1)} %rows.9) | copy-start | bytes 27033604
  30.3 4.3 %collective-permute-start.4 = (f32[8,128]{1,0:T(8,128)S(1)}, f32[8,128]{1,0:T(8,128)S(1)}, u32[]{:S(2)}, u32[]{:S(2)}) collective-permute-start(f32[8,128]{1,0:T(8,128)S(1)} %get-tuple-element.58), channel_id=1, source_target_pairs={{0,16},{16,0},{32,48},{48,32},{64,80},{80,64},{96,112},{112,96},{1... | collective-permute-start | bytes 12296 | tf_op jit(solution)/shard_map/ppermute | solution.py:76
  32.5 3.0 %collective-permute-start.5 = (f32[8,128]{1,0:T(8,128)S(1)}, f32[8,128]{1,0:T(8,128)S(1)}, u32[]{:S(2)}, u32[]{:S(2)}) collective-permute-start(f32[8,128]{1,0:T(8,128)S(1)} %get-tuple-element.59), channel_id=1, source_target_pairs={{16,32},{32,16},{48,64},{64,48},{80,96},{96,80},{112,128},{128,112... | collective-permute-start | bytes 12296 | tf_op jit(solution)/shard_map/ppermute | solution.py:76
  32.5 3.0 %collective-permute-start.6 = (f32[8,128]{1,0:T(8,128)S(1)}, f32[8,128]{1,0:T(8,128)S(1)}, u32[]{:S(2)}, u32[]{:S(2)}) collective-permute-start(f32[8,128]{1,0:T(8,128)S(1)} %get-tuple-element.60), channel_id=1, source_target_pairs={{0,1},{1,0},{2,3},{3,2},{4,5},{5,4},{6,7},{7,6},{8,9},{9,8},{10,11... | collective-permute-start | bytes 12296 | tf_op jit(solution)/shard_map/ppermute | solution.py:76
  33.8 5.8 %collective-permute-start.7 = (f32[8,128]{1,0:T(8,128)S(1)}, f32[8,128]{1,0:T(8,128)S(1)}, u32[]{:S(2)}, u32[]{:S(2)}) collective-permute-start(f32[8,128]{1,0:T(8,128)S(1)} %get-tuple-element.61), channel_id=1, source_target_pairs={{1,2},{2,1},{3,4},{4,3},{5,6},{6,5},{7,8},{8,7},{9,10},{10,9},{11,... | collective-permute-start | bytes 12296 | tf_op jit(solution)/shard_map/ppermute | solution.py:76
  41.9 23.1 %copy-start.2 = (f32[64,80]{1,0:T(8,128)}, f32[64,80]{1,0:T(8,128)S(1)}, u32[]{:S(2)}) copy-start(f32[64,80]{1,0:T(8,128)S(1)} %get-tuple-element.63.image) | copy-start | bytes 61444
  67.5 0.5 copy-start.6
